TPU v7x, 128 devices: a whole 4x4x4 slice. The times are simulated.
128 devices in a mesh: row: 8 (over y, core), col: 16 (over x, z).
Axes of the slice: x: 4, y: 4, z: 4, core: 2. Of those that a mesh axis runs over, the one named last changes fastest.
Arguments:
- features: bfloat16 [131072, 128], P(('row', 'col')), may hold values from -6 to 6
- weight: bfloat16 [128, 128], replicated, may hold values from -0.5 to 0.5
- adj_tiles: bfloat16 [12288, 128, 128], P(('row', 'col')), may hold values from -0.21875 to 0.21875
- tile_rows: int32 [12288], P(('row', 'col')), may hold values from 0 to 127
- tile_cols: int32 [12288], P(('row', 'col')), may hold values from 0 to 63
- tile_count: int32 [128], P(('row', 'col')), may hold values from 24 to 96, as said below
- cotangent: bfloat16 [131072, 128], P(('row', 'col')), may hold values from -6 to 6
Outputs:
- out_features: bfloat16 [131072, 128], P(('row', 'col'))
- weight_grad: float32 [128, 128], replicated
- feature_grad: bfloat16 [131072, 128], P(('row', 'col'))
Inputs may be any that keep to these rules, and one draw needn't show every extreme that they name: Each device has 96 slots, of which the first tile_count are in use; in every draw all devices of at least one row panel use all 96 slots.
All inputs are finite; a program needn't handle non-finite values.
Results may differ from a plain program's by a relative error of at most 0.019.
Values may be sent and summed in bfloat16 or wider, within the bound.
A program may use at most 128 MiB of HBM per device.

v0:
```python
import jax
import jax.numpy as jnp
from jax import lax
from jax.sharding import PartitionSpec as P


def sent_to_all(x, axis):
    copies = jnp.broadcast_to(x, (lax.axis_size(axis), *x.shape))
    return lax.all_to_all(copies, axis, split_axis=0, concat_axis=0, tiled=True)


def in_order(pieces, dim):
    pieces = jnp.moveaxis(pieces, 0, dim)
    shape = pieces.shape
    return pieces.reshape(*shape[:dim], shape[dim] * shape[dim + 1], *shape[dim + 2 :])


def gather_directly(x, axis, dim):
    pieces = sent_to_all(x, axis)
    return in_order(pieces, dim)


def over_pieces(x, axis):
    pieces = lax.all_gather(x, axis)
    return pieces.sum(axis=0)


def in_blocks(x, dim, length):
    before, after = (x.shape[:dim], x.shape[dim + 1 :])
    return jnp.moveaxis(x.reshape(*before, length, -1, *after), dim, 0)


def sent_and_summed(x, axis, dim):
    pieces = in_blocks(x, dim, lax.axis_size(axis))
    arrived = lax.all_to_all(pieces, axis, split_axis=0, concat_axis=0, tiled=True)
    return arrived.astype(jnp.float32).sum(axis=0)


def activate(value):
    return jax.nn.gelu(value, approximate=True)


def activate_grad(pre_act, upstream):
    _, pullback = jax.vjp(activate, pre_act)
    return pullback(upstream)[0]


def tile_pass(summed, tile_values, row_ids, col_ids, live_count, source, backward):
    slot_count = tile_values.shape[0]
    block_size = min(64, slot_count)

    def block_step(block_index, running):
        offset = jnp.minimum(block_index * block_size, slot_count - block_size)
        positions = offset + jnp.arange(block_size, dtype=jnp.int32)
        usable = (positions >= block_index * block_size) & (positions < live_count)
        chosen = lax.dynamic_slice_in_dim(tile_values, offset, block_size, 0)
        chosen = chosen * usable[:, None, None].astype(chosen.dtype)
        row_block = jnp.maximum(lax.dynamic_slice_in_dim(row_ids, offset, block_size, 0), 0)
        col_block = jnp.maximum(lax.dynamic_slice_in_dim(col_ids, offset, block_size, 0), 0)
        if backward:
            product = jnp.einsum(
                "bij,bif->bjf", chosen, source[row_block], preferred_element_type=jnp.float32
            )
            return running.at[col_block].add(product)
        product = jnp.einsum(
            "bij,bjf->bif", chosen, source[col_block], preferred_element_type=jnp.float32
        )
        return running.at[row_block].add(product)

    return lax.fori_loop(0, (live_count + block_size - 1) // block_size, block_step, summed)


def shards(features, weight, adj_tiles, tile_rows, tile_cols, tile_count, cotangent):
    node_dev, feature_width = features.shape
    tile_size = adj_tiles.shape[1]
    panel_tiles = lax.axis_size("col") * node_dev // tile_size
    group_tiles = lax.axis_size("row") * node_dev // tile_size
    live_count = tile_count[0]
    group_rows = gather_directly(features, "row", 0).reshape(group_tiles, tile_size, feature_width)
    summed = jnp.zeros((panel_tiles, tile_size, feature_width), jnp.float32)
    own_values, own_rows, own_cols, own_live = (adj_tiles, tile_rows, tile_cols, live_count)
    summed = tile_pass(summed, own_values, own_rows, own_cols, own_live, group_rows, False)
    panel_partial = summed.reshape(-1, feature_width)
    transposed = (((1,), (1,)), ((), ()))
    hidden = lax.psum_scatter(
        panel_partial.astype(jnp.bfloat16), "col", scatter_dimension=0, tiled=True
    )
    pre_act = jnp.dot(hidden, weight, preferred_element_type=jnp.float32)
    pre_grad = activate_grad(pre_act, cotangent.astype(jnp.float32)).astype(jnp.bfloat16)
    own_grad = lax.dot_general(
        pre_grad, weight, transposed, preferred_element_type=jnp.float32
    ).astype(jnp.bfloat16)
    hidden_grad = lax.all_gather(own_grad, "col", axis=0, tiled=True)
    out_features = activate(pre_act).astype(jnp.bfloat16)
    weight_term = lax.dot_general(
        hidden, pre_grad, (((0,), (0,)), ((), ())), preferred_element_type=jnp.float32
    )
    weight_grad = over_pieces(weight_term, ("row", "col"))
    grad_tiles = hidden_grad.reshape(panel_tiles, tile_size, feature_width)
    group_grads = jnp.zeros((group_tiles, tile_size, feature_width), jnp.float32)
    group_grads = tile_pass(group_grads, own_values, own_rows, own_cols, own_live, grad_tiles, True)
    feature_grad = sent_and_summed(
        group_grads.reshape(-1, feature_width).astype(jnp.bfloat16), "row", 0
    )
    return (out_features, weight_grad, feature_grad.astype(jnp.bfloat16))


def solution(mesh):
    in_specs = (
        P(("row", "col"), None),
        P(),
        P(("row", "col"), None, None),
        P(("row", "col")),
        P(("row", "col")),
        P(("row", "col")),
        P(("row", "col"), None),
    )
    out_specs = (P(("row", "col"), None), P(), P(("row", "col"), None))
    return jax.shard_map(shards, mesh=mesh, in_specs=in_specs, out_specs=out_specs, check_vma=False)
```

profile of v0, /device:TPU:1, one launch (start us, length us, event | category | flops | bytes accessed | tf_op | source)
XLA Modules:
  0.0 334.7 jit_solution(14545749617968887573)
XLA Ops:
  7.2 2.6 broadcast_in_dim.24
  9.7 6.0 %all-to-all-start = ((bf16[8,1024,128]{2,1,0:T(8,128)(2,1)}), bf16[8,1024,128]{2,1,0:T(8,128)(2,1)S(1)}, u32[]{:S(2)}, u32[]{:S(2)}) async-start(bf16[8,1024,128]{2,1,0:T(8,128)(2,1)} %broadcast_in_dim.24), calls=%async_computation | async-start | bytes 4194304 | tf_op jit(solution)/shard_map/all_to_all | solution.py:9
  16.4 25.7 %all-to-all-done = bf16[8,1024,128]{2,1,0:T(8,128)(2,1)S(1)} async-done(((bf16[8,1024,128]{2,1,0:T(8,128)(2,1)}), bf16[8,1024,128]{2,1,0:T(8,128)(2,1)S(1)}, u32[]{:S(2)}, u32[]{:S(2)}) %all-to-all-start) | async-done | bytes 2097184 | tf_op jit(solution)/shard_map/all_to_all | solution.py:9
  42.1 4.3 %broadcast_in_dim.23 = f32[128,128,128]{2,1,0:T(8,128)} broadcast(f32[]{:T(128)} %constant.58.clone.1), dimensions={} | broadcast | bytes 8388612 | tf_op jit(solution)/shard_map/broadcast_in_dim | solution.py:80
  46.4 45.1 %while.20 = (s32[]{:T(128)}, f32[128,128,128]{2,1,0:T(8,128)}, s32[]{:T(128)}, s32[96]{0:T(128)S(1)}, bf16[96,128,128]{2,1,0:T(8,128)(2,1)}, /*index=5*/s32[]{:T...) while((s32[]{:T(128)}, f32[128,128,128]{2,1,0:T(8,128)}, ...), condition=%wide.region_2.3_spmd, body=%wide.region_0.2_spmd.sunk | while | flops 270534080 | bytes 41949444 | solution.py:70
  46.4 1.2 copy-done.1
  47.7 2.5 gather_fusion
  50.9 4.3 %fusion.35 = f32[64,128,128]{2,1,0:T(8,128)} fusion(bf16[64,128,128]{2,1,0:T(8,128)(2,1)S(1)} %gather_fusion, bf16[96,128,128]{2,1,0:T(8,128)(2,1)} %get-tuple-element.275, s32[]{:T(128)S(6)} %select_n.23, bf16[64]{0:T(256)(128)(2,1)S(1)} %and_convert_fusion.4), kind=kOutput, calls=%fused_computation.4.clone.1 | convolution fusion | flops 269484032 | bytes 8388740 | tf_op jit(solution)/shard_map/while/body/bij,bjf->bif/dot_general | solution.py:65
  55.2 13.7 %scatter_fusion = f32[128,128,128]{2,1,0:T(8,128)} fusion(f32[128,128,128]{2,1,0:T(8,128)} %get-tuple-element.259, s32[64]{0:T(128)S(1)} %get-tuple-element.233, f32[64,128,128]{2,1,0:T(8,128)} %fusion.35), kind=kCustom, calls=%fused_computation.2.clone.1 | custom fusion | flops 1048576 | bytes 12583168 | tf_op jit(solution)/shard_map/while/body/scatter-add | solution.py:68
  69.0 1.2 copy-done.1
  70.2 2.5 gather_fusion
  73.4 4.3 %fusion.35 = f32[64,128,128]{2,1,0:T(8,128)} fusion(bf16[64,128,128]{2,1,0:T(8,128)(2,1)S(1)} %gather_fusion, bf16[96,128,128]{2,1,0:T(8,128)(2,1)} %get-tuple-element.275, s32[]{:T(128)S(6)} %select_n.23, bf16[64]{0:T(256)(128)(2,1)S(1)} %and_convert_fusion.4), kind=kOutput, calls=%fused_computation.4.clone.1 | convolution fusion | flops 269484032 | bytes 8388740 | tf_op jit(solution)/shard_map/while/body/bij,bjf->bif/dot_general | solution.py:65
  77.7 13.7 %scatter_fusion = f32[128,128,128]{2,1,0:T(8,128)} fusion(f32[128,128,128]{2,1,0:T(8,128)} %get-tuple-element.259, s32[64]{0:T(128)S(1)} %get-tuple-element.233, f32[64,128,128]{2,1,0:T(8,128)} %fusion.35), kind=kCustom, calls=%fused_computation.2.clone.1 | custom fusion | flops 1048576 | bytes 12583168 | tf_op jit(solution)/shard_map/while/body/scatter-add | solution.py:68
  91.4 6.3 %convert_element_type.43 = bf16[128,128,128]{2,1,0:T(8,128)(2,1)} convert(f32[128,128,128]{2,1,0:T(8,128)} %get-tuple-element.89) | non-fusion elementwise | flops 2097152 | bytes 12582912 | tf_op jit(solution)/shard_map/convert_element_type | solution.py:86
  97.8 75.7 %reduce-scatter.2.cloned.1.call-done = bf16[1024,128]{1,0:T(8,128)(2,1)} async-done(((bf16[16384,128]{1,0:T(8,128)(2,1)}), bf16[1024,128]{1,0:T(8,128)(2,1)}) %reduce-scatter.2.cloned.1.call-update) | async-done | bytes 262160 | tf_op jit(solution)/shard_map/reduce_scatter | solution.py:85
  173.5 2.3 fusion.10
  177.8 51.7 %all-gather.4.cloned.1.call-done = bf16[16384,128]{1,0:T(8,128)(2,1)} async-done(((bf16[1024,128]{1,0:T(8,128)(2,1)}), bf16[16384,128]{1,0:T(8,128)(2,1)}) %all-gather.4.cloned.1.call-update) | async-done | bytes 4194320 | tf_op jit(solution)/shard_map/all_gather | solution.py:93
  229.5 2.4 broadcast_in_dim.25
  231.9 56.7 %while.21 = (s32[]{:T(128)}, f32[64,128,128]{2,1,0:T(8,128)}, s32[]{:T(128)}, s32[96]{0:T(128)S(1)}, bf16[96,128,128]{2,1,0:T(8,128)(2,1)}, /*index=5*/s32[]{:T(...) while((s32[]{:T(128)}, f32[64,128,128]{2,1,0:T(8,128)}, ...), condition=%wide.region_7.8_spmd, body=%wide.region_5.7_spmd.sunk | while | flops 270534080 | bytes 33560776 | solution.py:70
  232.0 4.3 %gather_fusion.1 = bf16[64,128,128]{2,1,0:T(8,128)(2,1)} fusion(bf16[128,128,128]{2,1,0:T(8,128)(2,1)} %get-tuple-element.317, s32[1024]{0:T(1024)S(1)} %pad_clamp_fusion.5), kind=kCustom, calls=%fused_computation.1.clone.1 | custom fusion | bytes 4194560 | tf_op jit(solution)/shard_map/while/body/gather | solution.py:62
  236.3 1.7 constant_dynamic-slice_fusion.2
  238.1 2.9 copy.13
  241.7 4.9 %fusion.38 = f32[64,128,128]{2,1,0:T(8,128)} fusion(bf16[64,128,128]{2,1,0:T(8,128)(2,1)} %gather_fusion.1, bf16[64,128,128]{1,2,0:T(8,128)(2,1)} %copy.13, bf16[64]{0:T(256)(128)(2,1)S(1)} %and_convert_fusion.5), kind=kOutput, calls=%fused_computation.13.clone.1 | convolution fusion | flops 269484032 | bytes 8388736 | tf_op jit(solution)/shard_map/while/body/bij,bif->bjf/dot_general | solution.py:61
  246.6 13.7 %scatter_fusion.1 = f32[64,128,128]{2,1,0:T(8,128)} fusion(f32[64,128,128]{2,1,0:T(8,128)} %get-tuple-element.298, s32[64]{0:T(128)S(1)} %get-tuple-element.243, f32[64,128,128]{2,1,0:T(8,128)} %fusion.38), kind=kCustom, calls=%fused_computation.3.clone.1 | custom fusion | flops 1048576 | bytes 12583168 | tf_op jit(solution)/shard_map/while/body/scatter-add | solution.py:64
  260.4 4.3 %gather_fusion.1 = bf16[64,128,128]{2,1,0:T(8,128)(2,1)} fusion(bf16[128,128,128]{2,1,0:T(8,128)(2,1)} %get-tuple-element.317, s32[1024]{0:T(1024)S(1)} %pad_clamp_fusion.5), kind=kCustom, calls=%fused_computation.1.clone.1 | custom fusion | bytes 4194560 | tf_op jit(solution)/shard_map/while/body/gather | solution.py:62
  264.7 1.7 constant_dynamic-slice_fusion.2
  266.4 2.9 copy.13
  270.0 4.9 %fusion.38 = f32[64,128,128]{2,1,0:T(8,128)} fusion(bf16[64,128,128]{2,1,0:T(8,128)(2,1)} %gather_fusion.1, bf16[64,128,128]{1,2,0:T(8,128)(2,1)} %copy.13, bf16[64]{0:T(256)(128)(2,1)S(1)} %and_convert_fusion.5), kind=kOutput, calls=%fused_computation.13.clone.1 | convolution fusion | flops 269484032 | bytes 8388736 | tf_op jit(solution)/shard_map/while/body/bij,bif->bjf/dot_general | solution.py:61
  274.9 13.7 %scatter_fusion.1 = f32[64,128,128]{2,1,0:T(8,128)} fusion(f32[64,128,128]{2,1,0:T(8,128)} %get-tuple-element.298, s32[64]{0:T(128)S(1)} %get-tuple-element.243, f32[64,128,128]{2,1,0:T(8,128)} %fusion.38), kind=kCustom, calls=%fused_computation.3.clone.1 | custom fusion | flops 1048576 | bytes 12583168 | tf_op jit(solution)/shard_map/while/body/scatter-add | solution.py:64
  288.6 2.9 convert_element_type.49
  291.5 31.1 %all_to_all.10 = bf16[8,1024,128]{2,1,0:T(8,128)(2,1)S(1)} all-to-all(bf16[8,1024,128]{2,1,0:T(8,128)(2,1)S(1)} %bitcast.22), channel_id=1, replica_groups=mesh['row'=8,'col'=16] {'row'}, dimensions={0} | all-to-all | bytes 4194304 | tf_op jit(solution)/shard_map/all_to_all | solution.py:35
  323.7 4.4 %reduce_sum.21 = f32[128,128]{1,0:T(8,128)} reduce(f32[128,128,128]{2,1,0:T(8,128)} %bitcast.23, f32[]{:T(128)} %constant.58.clone.1), dimensions={0}, to_apply=%region_4.5 | reduce | flops 2080768 | bytes 8454148 | tf_op jit(solution)/shard_map/reduce_sum | solution.py:25
  (38 shorter events, 6.0 us)
Async XLA Ops:
  7.2 166.4 %copy-start = (bf16[128,128]{1,0:T(8,128)(2,1)S(1)}, bf16[128,128]{1,0:T(8,128)(2,1)}, u32[]{:S(2)}) copy-start(bf16[128,128]{1,0:T(8,128)(2,1)} %param.12) | copy-start | bytes 98308
  9.7 32.3 %all-to-all-start = ((bf16[8,1024,128]{2,1,0:T(8,128)(2,1)}), bf16[8,1024,128]{2,1,0:T(8,128)(2,1)S(1)}, u32[]{:S(2)}, u32[]{:S(2)}) async-start(bf16[8,1024,128]{2,1,0:T(8,128)(2,1)} %broadcast_in_dim.24), calls=%async_computation | async-start | bytes 4194304 | tf_op jit(solution)/shard_map/all_to_all | solution.py:9
  15.7 157.8 %reduce-scatter.2.cloned.1.call-start = ((), (), s32[]{:S(2)}) async-start(), calls=%async_computation.3 | async-start | bytes 4456448 | tf_op jit(solution)/shard_map/reduce_scatter | solution.py:85
  42.1 4.3 %copy-start.4 = (s32[96]{0:T(128)S(1)}, s32[96]{0:T(128)}, u32[]{:S(2)}) copy-start(s32[96]{0:T(128)} %param.14) | copy-start | bytes 1156
  42.1 4.3 %copy-start.5 = (s32[96]{0:T(128)S(1)}, s32[96]{0:T(128)}, u32[]{:S(2)}) copy-start(s32[96]{0:T(128)} %param.15) | copy-start | bytes 1156
  46.4 1.3 copy-start.1
  55.2 13.7 %copy-start.2 = (bf16[64,128,128]{2,1,0:T(8,128)(2,1)S(1)}, bf16[64,128,128]{2,1,0:T(8,128)(2,1)}, u32[]{:S(2)}) copy-start(bf16[64,128,128]{2,1,0:T(8,128)(2,1)} %copy-done.1) | copy-start | bytes 6291460 | tf_op jit(solution)/shard_map/while
  68.9 1.3 copy-start.1
  77.7 13.7 %copy-start.2 = (bf16[64,128,128]{2,1,0:T(8,128)(2,1)S(1)}, bf16[64,128,128]{2,1,0:T(8,128)(2,1)}, u32[]{:S(2)}) copy-start(bf16[64,128,128]{2,1,0:T(8,128)(2,1)} %copy-done.1) | copy-start | bytes 6291460 | tf_op jit(solution)/shard_map/while
  97.7 75.8 %copy-start.6 = (bf16[1024,128]{1,0:T(8,128)(2,1)S(1)}, bf16[1024,128]{1,0:T(8,128)(2,1)}, u32[]{:S(2)}) copy-start(bf16[1024,128]{1,0:T(8,128)(2,1)} %param.17) | copy-start | bytes 786436
  97.8 131.7 %all-gather.4.cloned.1.call-start = ((), (), s32[]{:S(2)}) async-start(), calls=%async_computation.4 | async-start | bytes 4456448 | tf_op jit(solution)/shard_map/all_gather | solution.py:93
  173.5 3.3 copy-start.3
  176.8 146.9 %all-gather.6.cloned.1.call-start = ((), (), s32[]{:S(2)}) async-start(), calls=%async_computation.5 | async-start | bytes 8454144 | tf_op jit(solution)/shard_map/all_gather | solution.py:24
Sparse Core Ops, SparseCore 0:
  97.9 75.6 reduce-scatter.1
  176.9 52.5 all-gather.3
  233.7 77.8 all-gather.5
where the time goes:
time: 336 us; the launch traced here: 335 us
  waiting for transfers between devices  153 us (46%)
  other arithmetic  72.3 us (22%)
  local copies, waits for them, and re-layouts  34.9 us (10%)
  blocking collectives  31.1 us (9%)
  matrix products  22.6 us (7%)
  between operations  14.4 us (4%)
  starting transfers between devices  6.06 us (2%)
    reduce_scatter x1, waiting for transfers between devices, shards(): lax.psum_scatter(panel_partial.astype(jnp.bfloat16), 'col', scatter_dimen...  75.7 us
    all_gather x1, waiting for transfers between devices, shards(): hidden_grad = lax.all_gather(own_grad, 'col', axis=0, tiled=True)  51.7 us
    all_to_all x1, blocking collectives, sent_and_summed(): lax.all_to_all(pieces, axis, split_axis=0, concat_axis=0, tiled=True)  31.1 us
    scatter-add x2, other arithmetic, block_step(): return running.at[row_block].add(product)  27.3 us
    scatter-add x2, other arithmetic, block_step(): return running.at[col_block].add(product)  27.3 us
    all_to_all x1, waiting for transfers between devices, sent_to_all(): return lax.all_to_all(copies, axis, split_axis=0, concat_axis=0, tiled=True)  25.7 us
    dot_general x2, matrix products, block_step(): jnp.einsum('bij,bif->bjf', chosen, source[row_block], preferred_element_t...  9.86 us
    dynamic_slice x4, local copies, waits for them, and re-layouts, block_step(): chosen = lax.dynamic_slice_in_dim(tile_values, offset, block_size, 0)  9.35 us
  transfers between devices with their start and end apart: 4, of which 3 were waited for; matrix products, arithmetic and copies ran while one was open for 19% of the time, Pallas kernels for 0%

commit v1 on v0

v1 whole, which is shorter than its diff:
```python
import jax
import jax.numpy as jnp
from jax import lax
from jax.experimental import pallas as pl
from jax.experimental.pallas import tpu as pltpu
from jax.sharding import PartitionSpec as P

MESH = pl.DeviceIdType.MESH
BF16, F32 = jnp.bfloat16, jnp.float32
VMEM_BYTES = 48 * 2**20
RING = 4
UNROLL = 8


class Links:
    def __init__(self, send_sem, recv_sem):
        self.send_sem, self.recv_sem, self.copies = send_sem, recv_sem, []

    def start(self, src, dst, device):
        at = len(self.copies)
        copy = pltpu.make_async_remote_copy(
            src_ref=src,
            dst_ref=dst,
            send_sem=self.send_sem.at[at],
            recv_sem=self.recv_sem.at[at],
            device_id=device,
            device_id_type=MESH,
        )
        copy.start()
        self.copies.append(copy)
        return copy

    def drain(self):
        for copy in self.copies:
            copy.wait_send()


class Axis:
    def __init__(self, position, device_at):
        self.position = position
        self.up = device_at(lax.rem(position + 1, RING))
        self.down = device_at(lax.rem(position + 3, RING))

    def at(self, offset):
        return lax.rem(self.position + offset, RING) if offset else self.position


class Place:
    def __init__(self):
        row, col = lax.axis_index("row"), lax.axis_index("col")
        self.row, self.col = row, col
        y, self.core = lax.div(row, 2), lax.rem(row, 2)
        x, z = lax.div(col, RING), lax.rem(col, RING)
        core = self.core
        self.y = Axis(y, lambda k: (k * 2 + core, col))
        self.x = Axis(x, lambda k: (row, k * RING + z))
        self.z = Axis(z, lambda k: (row, x * RING + k))
        self.sibling_row = row + 1 - 2 * core
        self.sibling = (self.sibling_row, col)

    def greet(self, axes, sibling):
        others = [d for axis in axes for d in (axis.up, axis.down)]
        if sibling:
            others.append(self.sibling)
        barrier = pltpu.get_barrier_semaphore()
        for other in others:
            pl.semaphore_signal(barrier, inc=1, device_id=other, device_id_type=MESH)
        pl.semaphore_wait(barrier, len(others))


class Sum4:
    def __init__(self, links, axis, part, buffers):
        self.links, self.axis, self.part = links, axis, part
        self.relay_up, self.relay_down, self.from_down, self.from_up = buffers
        half = self.relay_up.shape[0]
        self.low, self.high = pl.ds(0, half), pl.ds(half, half)

    def push_far(self):
        far = self.part(2)
        self.c_up = self.links.start(far.at[self.low], self.relay_up, self.axis.up)
        self.c_down = self.links.start(far.at[self.high], self.relay_down, self.axis.down)

    def push_up(self):
        self.n_up = self.links.start(
            self.part(1).at[self.high], self.from_down.at[self.high], self.axis.up
        )

    def push_down(self):
        self.n_down = self.links.start(
            self.part(3).at[self.low], self.from_up.at[self.low], self.axis.down
        )

    def push(self):
        self.push_far()
        self.push_up()
        self.push_down()

    def relay(self):
        self.c_up.wait_recv()
        mine = self.part(1)[self.low]
        self.relay_up[...] = (self.relay_up[...].astype(F32) + mine.astype(F32)).astype(BF16)
        self.r_up = self.links.start(self.relay_up, self.from_down.at[self.low], self.axis.up)
        self.c_down.wait_recv()
        mine = self.part(3)[self.high]
        self.relay_down[...] = (self.relay_down[...].astype(F32) + mine.astype(F32)).astype(BF16)
        self.r_down = self.links.start(
            self.relay_down, self.from_up.at[self.high], self.axis.down
        )

    def finish(self):
        for copy in (self.n_up, self.n_down, self.r_up, self.r_down):
            copy.wait_recv()
        return (
            self.part(0)[...].astype(F32)
            + self.from_down[...].astype(F32)
            + self.from_up[...].astype(F32)
        )


class Share4:
    def __init__(self, links, axis, slot, half):
        self.links, self.axis, self.slot = links, axis, slot
        self.low, self.high = pl.ds(0, half), pl.ds(half, half)

    def send(self, k, rows, device):
        ref = self.slot(k).at[rows]
        return self.links.start(ref, ref, device)

    def push(self):
        self.up_low = self.send(0, self.low, self.axis.up)
        self.down_high = self.send(0, self.high, self.axis.down)
        self.up_high = self.send(0, self.high, self.axis.up)
        self.down_low = self.send(0, self.low, self.axis.down)

    def relay(self):
        self.up_low.wait_recv()
        self.far_low = self.send(3, self.low, self.axis.up)
        self.down_high.wait_recv()
        self.far_high = self.send(1, self.high, self.axis.down)

    def near(self):
        self.up_high.wait_recv()
        self.down_low.wait_recv()

    def far(self):
        self.far_low.wait_recv()
        self.far_high.wait_recv()


def gather_row_kernel(own_ref, all_ref, send_sem, recv_sem):
    here = Place()
    here.greet([here.y], True)
    links = Links(send_sem, recv_sem)
    half = own_ref.shape[0] // 2
    all_ref[here.row] = own_ref[...]

    def slot(k):
        return all_ref.at[here.y.at(k) * 2 + here.core]

    share = Share4(links, here.y, slot, half)

    def across(k, rows):
        ref = slot(k).at[rows]
        return links.start(ref, ref, here.sibling)

    low, high = share.low, share.high
    share.push()
    twins = [across(0, low), across(0, high)]
    share.relay()
    twins += [across(3, low), across(1, high)]
    share.near()
    twins += [across(3, high), across(1, low)]
    share.far()
    twins += [across(2, low), across(2, high)]
    for copy in twins:
        copy.wait_recv()
    links.drain()


def tile_kernel(backward, count_ref, to_ref, from_ref, tiles_ref, source_ref, out_ref, total):
    total[...] = jnp.zeros_like(total)
    count = count_ref[0]
    contract = ((0,), (0,)) if backward else ((1,), (0,))

    def step(block, _):
        first = block * UNROLL
        products = []
        for k in range(UNROLL):
            product = lax.dot_general(
                tiles_ref[first + k],
                source_ref[from_ref[first + k]],
                (contract, ((), ())),
                preferred_element_type=F32,
            )
            products.append(jnp.where(first + k < count, product, 0.0))
        for k in range(UNROLL):
            total[to_ref[first + k]] += products[k]
        return 0

    lax.fori_loop(0, lax.div(count + UNROLL - 1, UNROLL), step, 0)
    out_ref[...] = total[...].astype(BF16)


def activation(value):
    root = 0.7978845608028654
    square = value * value
    t = jnp.tanh(root * (value + 0.044715 * (value * square)))
    half = 0.5 * (1.0 + t)
    slope = half + (0.5 * value) * (1.0 - t * t) * (root * (1.0 + 3.0 * 0.044715 * square))
    return value * half, slope


def middle_kernel(
    part_ref, weight_ref, cot_ref, out_ref, term_ref, grads_ref,
    relay_buf, from_buf, part2_buf, relay2_buf, from2_buf, hidden_buf, grad_buf, send_sem, recv_sem,
):
    here = Place()
    here.greet([here.x, here.z], False)
    links = Links(send_sem, recv_sem)
    rows = part_ref.shape[1] // 2
    quarter = rows // 2
    halves = (0, 1)
    slices = [pl.ds(h * rows, rows) for h in halves]
    firsts, seconds = (here.z, here.x), (here.x, here.z)

    def col_of(h, first, second):
        return second * RING + first if h == 0 else first * RING + second

    def sum_first(h, delta):
        first, second = firsts[h], seconds[h]

        def part(k):
            return part_ref.at[col_of(h, first.at(k), second.at(delta)), slices[h]]

        r, f = relay_buf.at[h, delta], from_buf.at[h, delta]
        return Sum4(links, first, part, (r.at[0], r.at[1], f.at[0], f.at[1]))

    def sum_second(h):
        r, f = relay2_buf.at[h], from2_buf.at[h]
        return Sum4(
            links, seconds[h], lambda k: part2_buf.at[h, k], (r.at[0], r.at[1], f.at[0], f.at[1])
        )

    sums = [[sum_first(h, d) for d in range(RING)] for h in halves]
    lasts = [sum_second(h) for h in halves]

    def done_first(h, d):
        part2_buf[h, d] = sums[h][d].finish().astype(part2_buf.dtype)

    for d in (2, 1):
        for h in halves:
            sums[h][d].push()
    for d, then in ((2, 3), (1, 0)):
        for h in halves:
            sums[h][d].relay()
        for h in halves:
            sums[h][then].push()
    for h in halves:
        done_first(h, 2)
        lasts[h].push_far()
    for d in (3, 0):
        for h in halves:
            sums[h][d].relay()
    for h in halves:
        done_first(h, 1)
        lasts[h].push_up()
        done_first(h, 3)
        lasts[h].push_down()
    for h in halves:
        lasts[h].relay()
    for h in halves:
        done_first(h, 0)

    weight = weight_ref[...]

    def dense(h):
        hidden = lasts[h].finish().astype(BF16)
        pre_act = jnp.dot(hidden, weight, preferred_element_type=F32)
        value, slope = activation(pre_act)
        pre_grad = (cot_ref[slices[h]].astype(F32) * slope).astype(BF16)
        own = lax.dot_general(
            pre_grad, weight, (((1,), (1,)), ((), ())), preferred_element_type=F32
        )
        grads_ref[here.col, slices[h]] = own.astype(BF16)
        out_ref[slices[h]] = value.astype(BF16)
        hidden_buf[slices[h]] = hidden
        grad_buf[slices[h]] = pre_grad

    def share_first(h):
        first, second = seconds[h], firsts[h]
        return Share4(
            links,
            first,
            lambda k: grads_ref.at[col_of(1 - h, first.at(k), second.position), slices[h]],
            quarter,
        )

    def share_second(h, delta):
        first, second = seconds[h], firsts[h]
        return Share4(
            links,
            second,
            lambda k: grads_ref.at[col_of(1 - h, first.at(delta), second.at(k)), slices[h]],
            quarter,
        )

    ones = [share_first(h) for h in halves]
    twos = [[share_second(h, d) for d in range(RING)] for h in halves]
    for h in halves:
        dense(h)
        ones[h].push()
        twos[h][0].push()
    term_ref[...] = lax.dot_general(
        hidden_buf[...], grad_buf[...], (((0,), (0,)), ((), ())), preferred_element_type=F32
    )
    for h in halves:
        ones[h].relay()
    for h in halves:
        ones[h].near()
        twos[h][0].relay()
        twos[h][1].push()
        twos[h][3].push()
    for h in halves:
        ones[h].far()
        twos[h][2].push()
    for d in (1, 3, 2):
        for h in halves:
            twos[h][d].relay()
    for d in (0, 1, 3, 2):
        for h in halves:
            twos[h][d].near()
            twos[h][d].far()
    links.drain()


def sum_row_kernel(part_ref, out_ref, own_buf, twin_buf, relay_buf, from_buf, send_sem, recv_sem):
    here = Place()
    here.greet([here.y], True)
    links = Links(send_sem, recv_sem)

    def block(k, core):
        return part_ref.at[here.y.at(k) * 2 + core]

    order = (2, 1, 3, 0)
    twins = {k: links.start(block(k, 1 - here.core), twin_buf.at[k], here.sibling) for k in order}
    total = Sum4(
        links,
        here.y,
        lambda k: own_buf.at[k],
        (relay_buf.at[0], relay_buf.at[1], from_buf.at[0], from_buf.at[1]),
    )
    pushes = {2: total.push_far, 1: total.push_up, 3: total.push_down}
    for k in order:
        twins[k].wait_recv()
        own_buf[k] = (block(k, here.core)[...].astype(F32) + twin_buf[k].astype(F32)).astype(
            own_buf.dtype
        )
        if k in pushes:
            pushes[k]()
    total.relay()
    out_ref[...] = total.finish().astype(BF16)
    links.drain()


def whole():
    return pl.BlockSpec(memory_space=pltpu.VMEM)


def small():
    return pl.BlockSpec(memory_space=pltpu.SMEM)


def semaphores(count):
    return [pltpu.SemaphoreType.DMA((count,))] * 2


def params(collective_id=None):
    if collective_id is None:
        return pltpu.CompilerParams(vmem_limit_bytes=VMEM_BYTES)
    return pltpu.CompilerParams(
        vmem_limit_bytes=VMEM_BYTES, collective_id=collective_id, has_side_effects=True
    )


def tile_pass(backward, count, to, source_ids, tiles, source, out_tiles):
    tile, width = source.shape[1:]
    return pl.pallas_call(
        lambda *refs: tile_kernel(backward, *refs),
        out_shape=jax.ShapeDtypeStruct((out_tiles, tile, width), BF16),
        in_specs=[small()] * 3 + [whole()] * 2,
        out_specs=whole(),
        scratch_shapes=[pltpu.VMEM((out_tiles, tile, width), F32)],
        compiler_params=params(),
        name="backward_tiles" if backward else "forward_tiles",
    )(count, to, source_ids, tiles, source)


def shards(features, weight, adj_tiles, tile_rows, tile_cols, tile_count, cotangent):
    nodes, width = features.shape
    tile = adj_tiles.shape[1]
    n_row, n_col = lax.axis_size("row"), lax.axis_size("col")
    panel_tiles, group_tiles = n_col * nodes // tile, n_row * nodes // tile
    half, quarter = nodes // 2, nodes // 4

    group = pl.pallas_call(
        gather_row_kernel,
        out_shape=jax.ShapeDtypeStruct((n_row, nodes, width), BF16),
        in_specs=[whole()],
        out_specs=whole(),
        scratch_shapes=semaphores(14),
        compiler_params=params(0),
        name="gather_row",
    )(features)
    partial = tile_pass(
        False, tile_count, tile_rows, tile_cols, adj_tiles,
        group.reshape(group_tiles, tile, width), panel_tiles,
    )
    out_features, term, grads = pl.pallas_call(
        middle_kernel,
        out_shape=(
            jax.ShapeDtypeStruct((nodes, width), BF16),
            jax.ShapeDtypeStruct((width, width), F32),
            jax.ShapeDtypeStruct((n_col, nodes, width), BF16),
        ),
        in_specs=[whole()] * 3,
        out_specs=(whole(),) * 3,
        scratch_shapes=[
            pltpu.VMEM((2, RING, 2, quarter, width), BF16),
            pltpu.VMEM((2, RING, 2, half, width), BF16),
            pltpu.VMEM((2, RING, half, width), BF16),
            pltpu.VMEM((2, 2, quarter, width), BF16),
            pltpu.VMEM((2, 2, half, width), BF16),
            pltpu.VMEM((nodes, width), BF16),
            pltpu.VMEM((nodes, width), BF16),
            *semaphores(120),
        ],
        compiler_params=params(1),
        name="middle",
    )(partial.reshape(n_col, nodes, width), weight, cotangent)
    weight_grad = lax.psum(term, ("row", "col"))
    sums = tile_pass(
        True, tile_count, tile_cols, tile_rows, adj_tiles,
        grads.reshape(panel_tiles, tile, width), group_tiles,
    )
    feature_grad = pl.pallas_call(
        sum_row_kernel,
        out_shape=jax.ShapeDtypeStruct((nodes, width), BF16),
        in_specs=[whole()],
        out_specs=whole(),
        scratch_shapes=[
            pltpu.VMEM((RING, nodes, width), BF16),
            pltpu.VMEM((RING, nodes, width), BF16),
            pltpu.VMEM((2, half, width), BF16),
            pltpu.VMEM((2, nodes, width), BF16),
            *semaphores(10),
        ],
        compiler_params=params(2),
        name="sum_row",
    )(sums.reshape(n_row, nodes, width))
    return (out_features, weight_grad, feature_grad)


def solution(mesh):
    in_specs = (
        P(("row", "col"), None),
        P(),
        P(("row", "col"), None, None),
        P(("row", "col")),
        P(("row", "col")),
        P(("row", "col")),
        P(("row", "col"), None),
    )
    out_specs = (P(("row", "col"), None), P(), P(("row", "col"), None))
    return jax.shard_map(shards, mesh=mesh, in_specs=in_specs, out_specs=out_specs, check_vma=False)
```

time: 336 us -> 239 us (0.71)
  Pallas kernels: 0 us -> 97.5 us
  other arithmetic: 72.3 us -> 0 us
  waiting for transfers between devices: 153 us -> 118 us
  blocking collectives: 31.1 us -> 0 us
  local copies, waits for them, and re-layouts: 34.9 us -> 8.98 us
  matrix products: 22.6 us -> 0 us
  starting transfers between devices: 6.06 us -> 0.04 us
    psum x0 -> x1, waiting for transfers between devices: none -> 118 us  [shards(): weight_grad = lax.psum(term, ('row', 'col'))]
    pallas_call x0 -> x5, Pallas kernels: none -> 97.5 us  [the longest x1 55.4 us: shards(): pl.pallas_call(middle_kernel, out_shape=(jax.ShapeDtypeStruct((nodes, wid...]
    reduce_scatter x1 -> x0, waiting for transfers between devices: 75.7 us -> none  [shards(): lax.psum_scatter(panel_partial.astype(jnp.bfloat16), 'col', scatter_dimen...]
    scatter-add x4 -> x0, other arithmetic: 54.7 us -> none  [the longest x2 27.3 us: block_step(): return running.at[row_block].add(product)]
    all_gather x2 -> x0, waiting for transfers between devices: 51.7 us -> none  [the longest x1 51.7 us: shards(): hidden_grad = lax.all_gather(own_grad, 'col', axis=0, tiled=True)]
    all_to_all x1 -> x0, blocking collectives: 31.1 us -> none  [sent_and_summed(): lax.all_to_all(pieces, axis, split_axis=0, concat_axis=0, tiled=True)]
    all_to_all x1 -> x0, waiting for transfers between devices: 25.7 us -> none  [sent_to_all(): return lax.all_to_all(copies, axis, split_axis=0, concat_axis=0, tiled=True)]
    dot_general x7 -> x0, matrix products: 22.6 us -> none  [the longest x2 9.86 us: block_step(): jnp.einsum('bij,bif->bjf', chosen, source[row_block], preferred_element_t...]
  transfers between devices with their start and end apart: 4 -> 1, of which waited for: 3 -> 1; matrix products, arithmetic and copies ran while one was open for 19% -> 0% of each run, Pallas kernels for 0% -> 9%
where the time goes in v1:
time: 239 us
  waiting for transfers between devices  118 us (49%)
  Pallas kernels  97.5 us (41%)
  between operations  14.8 us (6%)
  local copies, waits for them, and re-layouts  8.98 us (4%)
    psum x1, waiting for transfers between devices, shards(): weight_grad = lax.psum(term, ('row', 'col'))  118 us
    pallas_call x1, Pallas kernels, shards(): pl.pallas_call(middle_kernel, out_shape=(jax.ShapeDtypeStruct((nodes, wid...  55.4 us
    pallas_call x1, Pallas kernels, shards(): pl.pallas_call(sum_row_kernel, out_shape=jax.ShapeDtypeStruct((nodes, wid...  17.7 us
    pallas_call x1, Pallas kernels, shards(): pl.pallas_call(gather_row_kernel, out_shape=jax.ShapeDtypeStruct((n_row,...  15.6 us
    unnamed x23, local copies, waits for them, and re-layouts  8.98 us
    pallas_call x2, Pallas kernels, tile_pass(): pl.pallas_call(lambda *refs: tile_kernel(backward, *refs), out_shape=jax....  8.65 us
  transfers between devices with their start and end apart: 1, of which 1 were waited for; matrix products, arithmetic and copies ran while one was open for 0% of the time, Pallas kernels for 9%

profile of v1, /device:TPU:1, one launch (start us, length us, event | category | flops | bytes accessed | tf_op | source)
XLA Modules:
  0.0 238.8 jit_solution(10965761750189146944)
XLA Ops:
  7.2 0.0 all-reduce.2.cloned.1.call-start
  7.9 0.0 copy-start.3
  7.9 0.9 copy-done.3
  8.8 15.6 %gather_row.1 = bf16[8,1024,128]{2,1,0:T(8,128)(2,1)S(1)} custom-call(bf16[1024,128]{1,0:T(8,128)(2,1)S(1)} %copy-done.3), custom_call_target="tpu_custom_call" | custom-call | tf_op jit(solution)/shard_map/gather_row/pallas_call | solution.py:405
  24.5 0.0 copy-start
  24.5 1.9 copy-done
  26.4 0.0 copy-start.6
  26.4 0.7 copy-done.6
  27.0 0.0 copy-start.8
  27.0 0.7 copy-done.8
  27.7 0.0 copy-start.4
  27.7 0.0 copy-start.5
  27.7 4.6 %forward_tiles.1 = bf16[128,128,128]{2,1,0:T(8,128)(2,1)} custom-call(s32[1]{0:T(128)S(6)} %copy.14.refs_0_, s32[96]{0:T(128)S(1)} %copy-done.6, s32[96]{0:T(128)S(1)} %copy-done.8, bf16[96,128,128]{2,1,0:T(8,128)(2,1)S(1)} %copy-done, bf16[64,128,128]{2,1,0:T(8,128)(2,1)S(1)} %bitcast.5), custom_call_target="tpu_custom_call" | custom-call | tf_op jit(solution)/shard_map/forward_tiles/pallas_call | solution.py:387
  32.3 0.0 copy-start.1
  32.3 0.0 copy-start.7
  32.3 0.0 copy-start.9
  32.3 0.0 copy-done.4
  32.3 0.0 copy-done.5
  32.3 55.4 %middle.1 = (bf16[1024,128]{1,0:T(8,128)(2,1)S(1)}, f32[128,128]{1,0:T(8,128)}, bf16[16,1024,128]{2,1,0:T(8,128)(2,1)S(1)}) custom-call(bf16[16,1024,128]{2,1,0:T(8,128)(2,1)} %bitcast.7, bf16[128,128]{1,0:T(8,128)(2,1)S(1)} %copy-done.5, bf16[1024,128]{1,0:T(8,128)(2,1)S(1)} %copy-done.4), custom_call_target="tpu_custom_call" | custom-call | tf_op jit(solution)/shard_map/middle/pallas_call | solution.py:418
  87.8 0.0 copy-start.2
  87.8 1.9 copy-done.2
  89.7 0.0 all-reduce.2.cloned.1.call-update
  89.7 0.0 copy-done.1
  89.8 0.0 copy-done.7
  89.8 0.0 copy-done.9
  89.8 4.0 %backward_tiles.1 = bf16[64,128,128]{2,1,0:T(8,128)(2,1)S(1)} custom-call(s32[1]{0:T(128)S(6)} %copy.14.refs_0_, s32[96]{0:T(128)S(1)} %copy-done.9, s32[96]{0:T(128)S(1)} %copy-done.7, bf16[96,128,128]{2,1,0:T(8,128)(2,1)S(1)} %copy-done.1, bf16[128,128,128]{2,1,0:T(8,128)(2,1)} %bitcast.6), custom_call_target="tpu_custom_call" | custom-call | tf_op jit(solution)/shard_map/backward_tiles/pallas_call | solution.py:387
  93.8 17.7 %sum_row.1 = bf16[1024,128]{1,0:T(8,128)(2,1)S(1)} custom-call(bf16[8,1024,128]{2,1,0:T(8,128)(2,1)S(1)} %bitcast.4), custom_call_target="tpu_custom_call" | custom-call | tf_op jit(solution)/shard_map/sum_row/pallas_call | solution.py:445
  111.5 117.5 %all-reduce.2.cloned.1.call-done = f32[128,128]{1,0:T(8,128)} async-done(((f32[128,128]{1,0:T(8,128)}), f32[128,128]{1,0:T(8,128)}) %all-reduce.2.cloned.1.call-update) | async-done | bytes 65552 | tf_op jit(solution)/shard_map/psum | solution.py:440
  229.1 0.7 copy.15
  229.8 1.5 copy.16
  231.2 0.7 copy.17
Async XLA Ops:
  7.2 221.9 %all-reduce.2.cloned.1.call-start = ((), (), s32[]{:S(2)}) async-start(), calls=%async_computation | async-start | bytes 131072 | tf_op jit(solution)/shard_map/psum | solution.py:440
  7.9 1.0 copy-start.3
  24.5 1.9 copy-start
  26.4 0.7 copy-start.6
  27.0 0.7 copy-start.8
  27.7 4.6 %copy-start.4 = (bf16[1024,128]{1,0:T(8,128)(2,1)S(1)}, bf16[1024,128]{1,0:T(8,128)(2,1)}, u32[]{:S(2)}) copy-start(bf16[1024,128]{1,0:T(8,128)(2,1)} %cot_ref.1) | copy-start | bytes 786436
  27.7 4.6 %copy-start.5 = (bf16[128,128]{1,0:T(8,128)(2,1)S(1)}, bf16[128,128]{1,0:T(8,128)(2,1)}, u32[]{:S(2)}) copy-start(bf16[128,128]{1,0:T(8,128)(2,1)} %weight_ref.1) | copy-start | bytes 98308
  32.3 57.5 %copy-start.1 = (bf16[96,128,128]{2,1,0:T(8,128)(2,1)S(1)}, bf16[96,128,128]{2,1,0:T(8,128)(2,1)}, u32[]{:S(2)}) copy-start(bf16[96,128,128]{2,1,0:T(8,128)(2,1)} %refs_3_.3) | copy-start | bytes 9437188
  32.3 57.5 %copy-start.7 = (s32[96]{0:T(128)S(1)}, s32[96]{0:T(128)}, u32[]{:S(2)}) copy-start(s32[96]{0:T(128)} %refs_2_.3) | copy-start | bytes 1156
  32.3 57.5 %copy-start.9 = (s32[96]{0:T(128)S(1)}, s32[96]{0:T(128)}, u32[]{:S(2)}) copy-start(s32[96]{0:T(128)} %refs_1_.3) | copy-start | bytes 1156
  87.8 2.0 copy-start.2
Sparse Core Ops, SparseCore 0:
  89.9 139.1 all-reduce.1

commit v2 on v1

--- a/solution.py
+++ b/solution.py
@@ -40,6 +40,9 @@
         self.position = position
         self.up = device_at(lax.rem(position + 1, RING))
         self.down = device_at(lax.rem(position + 3, RING))
+        odd = lax.rem(position, 2)
+        self.pair = device_at(position + 1 - 2 * odd)
+        self.other_pair = device_at(lax.rem(position + 3 + 2 * odd, RING))
 
     def at(self, offset):
         return lax.rem(self.position + offset, RING) if offset else self.position
@@ -68,6 +71,10 @@
         pl.semaphore_wait(barrier, len(others))
 
 
+def add_to(ref, value):
+    ref[...] = (ref[...].astype(F32) + value.astype(F32)).astype(ref.dtype)
+
+
 class Sum4:
     def __init__(self, links, axis, part, buffers):
         self.links, self.axis, self.part = links, axis, part
@@ -98,11 +105,11 @@
     def relay(self):
         self.c_up.wait_recv()
         mine = self.part(1)[self.low]
-        self.relay_up[...] = (self.relay_up[...].astype(F32) + mine.astype(F32)).astype(BF16)
+        add_to(self.relay_up, mine)
         self.r_up = self.links.start(self.relay_up, self.from_down.at[self.low], self.axis.up)
         self.c_down.wait_recv()
         mine = self.part(3)[self.high]
-        self.relay_down[...] = (self.relay_down[...].astype(F32) + mine.astype(F32)).astype(BF16)
+        add_to(self.relay_down, mine)
         self.r_down = self.links.start(
             self.relay_down, self.from_up.at[self.high], self.axis.down
         )
@@ -145,6 +152,42 @@
     def far(self):
         self.far_low.wait_recv()
         self.far_high.wait_recv()
+
+
+class SumAll:
+    def __init__(self, links, here, term, result, relay, came, own, got):
+        x = here.x
+        self.links, self.own, self.got = links, own, got
+        self.ring = Sum4(
+            links, x, lambda k: term.at[x.at(k)], (relay.at[0], relay.at[1], came.at[0], came.at[1])
+        )
+        self.share = Share4(links, x, lambda k: result.at[x.at(k)], result.shape[1] // 2)
+        self.slot = result.at[x.position]
+        pairs = (here.z.pair, here.z.other_pair, here.y.pair, here.y.other_pair, here.sibling)
+        self.steps = self.run(pairs)
+
+    def run(self, pairs):
+        self.ring.push()
+        yield
+        self.ring.relay()
+        yield
+        total = self.ring.finish()
+        for at, pair in enumerate(pairs):
+            self.own[at] = total
+            copy = self.links.start(self.own.at[at], self.got.at[at], pair)
+            yield
+            copy.wait_recv()
+            total = self.own[at] + self.got[at]
+        self.slot[...] = total
+        self.share.push()
+        yield
+        self.share.relay()
+        yield
+        self.share.near()
+        self.share.far()
+
+    def next(self):
+        next(self.steps, None)
 
 
 def gather_row_kernel(own_ref, all_ref, send_sem, recv_sem):
@@ -211,11 +254,12 @@
 
 
 def middle_kernel(
-    part_ref, weight_ref, cot_ref, out_ref, term_ref, grads_ref,
-    relay_buf, from_buf, part2_buf, relay2_buf, from2_buf, hidden_buf, grad_buf, send_sem, recv_sem,
+    part_ref, weight_ref, cot_ref, out_ref, weight_grad_ref, grads_ref,
+    relay_buf, from_buf, part2_buf, relay2_buf, from2_buf, hidden_buf, grad_buf,
+    term_buf, term_relay, term_from, term_own, term_got, send_sem, recv_sem,
 ):
     here = Place()
-    here.greet([here.x, here.z], False)
+    here.greet([here.x, here.y, here.z], True)
     links = Links(send_sem, recv_sem)
     rows = part_ref.shape[1] // 2
     quarter = rows // 2
@@ -310,26 +354,36 @@
         dense(h)
         ones[h].push()
         twos[h][0].push()
-    term_ref[...] = lax.dot_general(
+    term = lax.dot_general(
         hidden_buf[...], grad_buf[...], (((0,), (0,)), ((), ())), preferred_element_type=F32
     )
+    term_buf[...] = term.reshape(term_buf.shape)
+    total = SumAll(
+        links, here, term_buf, weight_grad_ref, term_relay, term_from, term_own, term_got
+    )
+    total.next()
     for h in halves:
         ones[h].relay()
+    total.next()
     for h in halves:
         ones[h].near()
         twos[h][0].relay()
         twos[h][1].push()
         twos[h][3].push()
+    total.next()
     for h in halves:
         ones[h].far()
         twos[h][2].push()
+    total.next()
     for d in (1, 3, 2):
         for h in halves:
             twos[h][d].relay()
+        total.next()
     for d in (0, 1, 3, 2):
         for h in halves:
             twos[h][d].near()
             twos[h][d].far()
+        total.next()
     links.drain()
 
 
@@ -415,11 +469,11 @@
         False, tile_count, tile_rows, tile_cols, adj_tiles,
         group.reshape(group_tiles, tile, width), panel_tiles,
     )
-    out_features, term, grads = pl.pallas_call(
+    out_features, weight_grad, grads = pl.pallas_call(
         middle_kernel,
         out_shape=(
             jax.ShapeDtypeStruct((nodes, width), BF16),
-            jax.ShapeDtypeStruct((width, width), F32),
+            jax.ShapeDtypeStruct((RING, width // RING, width), F32),
             jax.ShapeDtypeStruct((n_col, nodes, width), BF16),
         ),
         in_specs=[whole()] * 3,
@@ -432,12 +486,16 @@
             pltpu.VMEM((2, 2, half, width), BF16),
             pltpu.VMEM((nodes, width), BF16),
             pltpu.VMEM((nodes, width), BF16),
-            *semaphores(120),
+            pltpu.VMEM((RING, width // RING, width), F32),
+            pltpu.VMEM((2, width // RING // 2, width), F32),
+            pltpu.VMEM((2, width // RING, width), F32),
+            pltpu.VMEM((5, width // RING, width), F32),
+            pltpu.VMEM((5, width // RING, width), F32),
+            *semaphores(137),
         ],
         compiler_params=params(1),
         name="middle",
     )(partial.reshape(n_col, nodes, width), weight, cotangent)
-    weight_grad = lax.psum(term, ("row", "col"))
     sums = tile_pass(
         True, tile_count, tile_cols, tile_rows, adj_tiles,
         grads.reshape(panel_tiles, tile, width), group_tiles,
@@ -457,7 +515,7 @@
         compiler_params=params(2),
         name="sum_row",
     )(sums.reshape(n_row, nodes, width))
-    return (out_features, weight_grad, feature_grad)
+    return (out_features, weight_grad.reshape(width, width), feature_grad)
 
 
 def solution(mesh):

time: 239 us -> 115 us (0.48)
  waiting for transfers between devices: 118 us -> 0 us
  between operations: 14.8 us -> 1.35 us
  Pallas kernels: 97.5 us -> 105 us
    psum x1 -> x0, waiting for transfers between devices: 118 us -> none  [shards(): weight_grad = lax.psum(term, ('row', 'col'))]
    pallas_call x1, Pallas kernels: 55.4 us -> 66 us  [shards(): pl.pallas_call(middle_kernel, out_shape=(jax.ShapeDtypeStruct((nodes, wid...]
    pallas_call x1, Pallas kernels: 17.7 us -> 11.5 us  [shards(): pl.pallas_call(sum_row_kernel, out_shape=jax.ShapeDtypeStruct((nodes, wid...]
    pallas_call x2, Pallas kernels: 8.65 us -> 12.3 us  [tile_pass(): pl.pallas_call(lambda *refs: tile_kernel(backward, *refs), out_shape=jax....]
  transfers between devices with their start and end apart: 1 -> 0, of which waited for: 1 -> 0; matrix products, arithmetic and copies ran while one was open for 0% -> 0% of each run, Pallas kernels for 9% -> 0%
where the time goes in v2:
time: 115 us
  Pallas kernels  105 us (91%)
  local copies, waits for them, and re-layouts  8.13 us (7%)
  between operations  1.35 us (1%)
    pallas_call x1, Pallas kernels, shards(): pl.pallas_call(middle_kernel, out_shape=(jax.ShapeDtypeStruct((nodes, wid...  66 us
    pallas_call x1, Pallas kernels, shards(): pl.pallas_call(gather_row_kernel, out_shape=jax.ShapeDtypeStruct((n_row,...  15.6 us
    pallas_call x2, Pallas kernels, tile_pass(): pl.pallas_call(lambda *refs: tile_kernel(backward, *refs), out_shape=jax....  12.3 us
    pallas_call x1, Pallas kernels, shards(): pl.pallas_call(sum_row_kernel, out_shape=jax.ShapeDtypeStruct((nodes, wid...  11.5 us
    unnamed x23, local copies, waits for them, and re-layouts  8.13 us

profile of v2, /device:TPU:1, one launch (start us, length us, event | category | flops | bytes accessed | tf_op | source)
XLA Modules:
  0.0 114.9 jit_solution(2055752204665994073)
XLA Ops:
  1.3 0.0 copy-start.3
  1.3 0.9 copy-done.3
  2.2 15.6 %gather_row.1 = bf16[8,1024,128]{2,1,0:T(8,128)(2,1)S(1)} custom-call(bf16[1024,128]{1,0:T(8,128)(2,1)S(1)} %copy-done.3), custom_call_target="tpu_custom_call" | custom-call | tf_op jit(solution)/shard_map/gather_row/pallas_call | solution.py:459
  17.9 0.0 copy-start
  17.9 1.9 %copy-done = bf16[96,128,128]{2,1,0:T(8,128)(2,1)S(1)} copy-done((bf16[96,128,128]{2,1,0:T(8,128)(2,1)S(1)}, bf16[96,128,128]{2,1,0:T(8,128)(2,1)}, u32[]{:S(2)}) %copy-start) | copy-done | bytes 3145752
  19.8 0.0 copy-start.6
  19.8 0.7 copy-done.6
  20.4 0.0 copy-start.8
  20.4 0.7 copy-done.8
  21.1 0.0 copy-start.4
  21.1 0.0 copy-start.5
  21.1 6.3 %forward_tiles.1 = bf16[128,128,128]{2,1,0:T(8,128)(2,1)} custom-call(s32[1]{0:T(128)S(6)} %copy.13.refs_0_, s32[96]{0:T(128)S(1)} %copy-done.6, s32[96]{0:T(128)S(1)} %copy-done.8, bf16[96,128,128]{2,1,0:T(8,128)(2,1)S(1)} %copy-done, bf16[64,128,128]{2,1,0:T(8,128)(2,1)S(1)} %bitcast.6), custom_call_target="tpu_custom_call" | custom-call | tf_op jit(solution)/shard_map/forward_tiles/pallas_call | solution.py:441
  27.4 0.0 copy-start.1
  27.4 0.0 copy-start.7
  27.4 0.0 copy-start.9
  27.4 0.0 copy-done.4
  27.4 0.0 copy-done.5
  27.4 66.0 %middle.1 = (bf16[1024,128]{1,0:T(8,128)(2,1)S(1)}, f32[4,32,128]{2,1,0:T(8,128)S(1)}, bf16[16,1024,128]{2,1,0:T(8,128)(2,1)S(1)}) custom-call(bf16[16,1024,128]{2,1,0:T(8,128)(2,1)} %bitcast.9, bf16[128,128]{1,0:T(8,128)(2,1)S(1)} %copy-done.5, bf16[1024,128]{1,0:T(8,128)(2,1)S(1)} %copy-done.4), custom_call_target="tpu_custom_call" | custom-call | tf_op jit(solution)/shard_map/middle/pallas_call | solution.py:472
  93.4 0.0 copy-start.2
  93.4 1.9 %copy-done.2 = bf16[16,1024,128]{2,1,0:T(8,128)(2,1)} copy-done((bf16[16,1024,128]{2,1,0:T(8,128)(2,1)}, bf16[16,1024,128]{2,1,0:T(8,128)(2,1)S(1)}, u32[]{:S(2)}) %copy-start.2) | copy-done | bytes 4194328
  95.4 0.0 copy-done.1
  95.4 0.0 copy-done.7
  95.4 0.0 copy-done.9
  95.4 6.0 %backward_tiles.1 = bf16[64,128,128]{2,1,0:T(8,128)(2,1)S(1)} custom-call(s32[1]{0:T(128)S(6)} %copy.13.refs_0_, s32[96]{0:T(128)S(1)} %copy-done.9, s32[96]{0:T(128)S(1)} %copy-done.7, bf16[96,128,128]{2,1,0:T(8,128)(2,1)S(1)} %copy-done.1, bf16[128,128,128]{2,1,0:T(8,128)(2,1)} %bitcast.7), custom_call_target="tpu_custom_call" | custom-call | tf_op jit(solution)/shard_map/backward_tiles/pallas_call | solution.py:441
  101.4 11.5 %sum_row.1 = bf16[1024,128]{1,0:T(8,128)(2,1)S(1)} custom-call(bf16[8,1024,128]{2,1,0:T(8,128)(2,1)S(1)} %bitcast.5), custom_call_target="tpu_custom_call" | custom-call | tf_op jit(solution)/shard_map/sum_row/pallas_call | solution.py:503
  112.9 0.7 copy.14
  113.6 0.6 copy.15
  114.2 0.7 copy.16
Async XLA Ops:
  1.3 1.0 copy-start.3
  17.9 1.9 %copy-start = (bf16[96,128,128]{2,1,0:T(8,128)(2,1)S(1)}, bf16[96,128,128]{2,1,0:T(8,128)(2,1)}, u32[]{:S(2)}) copy-start(bf16[96,128,128]{2,1,0:T(8,128)(2,1)} %refs_3_.3) | copy-start | bytes 9437188
  19.8 0.7 copy-start.6
  20.4 0.7 copy-start.8
  21.1 6.3 %copy-start.4 = (bf16[1024,128]{1,0:T(8,128)(2,1)S(1)}, bf16[1024,128]{1,0:T(8,128)(2,1)}, u32[]{:S(2)}) copy-start(bf16[1024,128]{1,0:T(8,128)(2,1)} %cot_ref.1) | copy-start | bytes 786436
  21.1 6.3 %copy-start.5 = (bf16[128,128]{1,0:T(8,128)(2,1)S(1)}, bf16[128,128]{1,0:T(8,128)(2,1)}, u32[]{:S(2)}) copy-start(bf16[128,128]{1,0:T(8,128)(2,1)} %weight_ref.1) | copy-start | bytes 98308
  27.4 68.0 %copy-start.1 = (bf16[96,128,128]{2,1,0:T(8,128)(2,1)S(1)}, bf16[96,128,128]{2,1,0:T(8,128)(2,1)}, u32[]{:S(2)}) copy-start(bf16[96,128,128]{2,1,0:T(8,128)(2,1)} %refs_3_.3) | copy-start | bytes 9437188
  27.4 68.0 %copy-start.7 = (s32[96]{0:T(128)S(1)}, s32[96]{0:T(128)}, u32[]{:S(2)}) copy-start(s32[96]{0:T(128)} %refs_2_.3) | copy-start | bytes 1156
  27.4 68.0 %copy-start.9 = (s32[96]{0:T(128)S(1)}, s32[96]{0:T(128)}, u32[]{:S(2)}) copy-start(s32[96]{0:T(128)} %refs_1_.3) | copy-start | bytes 1156
  93.4 1.9 %copy-start.2 = (bf16[16,1024,128]{2,1,0:T(8,128)(2,1)}, bf16[16,1024,128]{2,1,0:T(8,128)(2,1)S(1)}, u32[]{:S(2)}) copy-start(bf16[16,1024,128]{2,1,0:T(8,128)(2,1)S(1)} %get-tuple-element.8) | copy-start | bytes 12582916

commit v3 on v2

v3 whole, which is shorter than its diff:
```python
import jax
import jax.numpy as jnp
from jax import lax
from jax.experimental import pallas as pl
from jax.experimental.pallas import tpu as pltpu
from jax.sharding import PartitionSpec as P

MESH = pl.DeviceIdType.MESH
BF16, F32 = jnp.bfloat16, jnp.float32
VMEM_BYTES = 63 * 2**20
RING = 4
UNROLL = 8


class Links:
    def __init__(self, send_sem, recv_sem):
        self.send_sem, self.recv_sem, self.copies = send_sem, recv_sem, []

    def start(self, src, dst, device):
        at = len(self.copies)
        copy = pltpu.make_async_remote_copy(
            src_ref=src,
            dst_ref=dst,
            send_sem=self.send_sem.at[at],
            recv_sem=self.recv_sem.at[at],
            device_id=device,
            device_id_type=MESH,
        )
        copy.start()
        self.copies.append(copy)
        return copy

    def drain(self):
        for copy in self.copies:
            copy.wait_send()


class Axis:
    def __init__(self, position, device_at):
        self.position = position
        self.up = device_at(lax.rem(position + 1, RING))
        self.down = device_at(lax.rem(position + 3, RING))
        odd = lax.rem(position, 2)
        self.pair = device_at(position + 1 - 2 * odd)
        self.other_pair = device_at(lax.rem(position + 3 + 2 * odd, RING))

    def at(self, offset):
        return lax.rem(self.position + offset, RING) if offset else self.position


class Place:
    def __init__(self):
        row, col = lax.axis_index("row"), lax.axis_index("col")
        self.row, self.col = row, col
        y, self.core = lax.div(row, 2), lax.rem(row, 2)
        x, z = lax.div(col, RING), lax.rem(col, RING)
        core = self.core
        self.y = Axis(y, lambda k: (k * 2 + core, col))
        self.x = Axis(x, lambda k: (row, k * RING + z))
        self.z = Axis(z, lambda k: (row, x * RING + k))
        self.sibling_row = row + 1 - 2 * core
        self.sibling = (self.sibling_row, col)

    def greet(self):
        barrier = pltpu.get_barrier_semaphore()
        others = [d for axis in (self.x, self.y, self.z) for d in (axis.up, axis.down)]
        others.append(self.sibling)
        for other in others:
            pl.semaphore_signal(barrier, inc=1, device_id=other, device_id_type=MESH)
        return lambda: pl.semaphore_wait(barrier, len(others))


def add_to(ref, value):
    ref[...] = (ref[...].astype(F32) + value.astype(F32)).astype(ref.dtype)


class Sum4:
    def __init__(self, links, axis, part, buffers):
        self.links, self.axis, self.part = links, axis, part
        self.relay_up, self.relay_down, self.from_down, self.from_up = buffers
        half = self.relay_up.shape[0]
        self.low, self.high = pl.ds(0, half), pl.ds(half, half)

    def push_far(self):
        far = self.part(2)
        self.c_up = self.links.start(far.at[self.low], self.relay_up, self.axis.up)
        self.c_down = self.links.start(far.at[self.high], self.relay_down, self.axis.down)

    def push_up(self):
        self.n_up = self.links.start(
            self.part(1).at[self.high], self.from_down.at[self.high], self.axis.up
        )

    def push_down(self):
        self.n_down = self.links.start(
            self.part(3).at[self.low], self.from_up.at[self.low], self.axis.down
        )

    def push(self):
        self.push_far()
        self.push_up()
        self.push_down()

    def relay(self):
        self.c_up.wait_recv()
        mine = self.part(1)[self.low]
        add_to(self.relay_up, mine)
        self.r_up = self.links.start(self.relay_up, self.from_down.at[self.low], self.axis.up)
        self.c_down.wait_recv()
        mine = self.part(3)[self.high]
        add_to(self.relay_down, mine)
        self.r_down = self.links.start(
            self.relay_down, self.from_up.at[self.high], self.axis.down
        )

    def finish(self):
        for copy in (self.n_up, self.n_down, self.r_up, self.r_down):
            copy.wait_recv()
        return (
            self.part(0)[...].astype(F32)
            + self.from_down[...].astype(F32)
            + self.from_up[...].astype(F32)
        )


class Share4:
    def __init__(self, links, axis, slot, half):
        self.links, self.axis, self.slot = links, axis, slot
        self.low, self.high = pl.ds(0, half), pl.ds(half, half)

    def send(self, k, rows, device):
        ref = self.slot(k).at[rows]
        return self.links.start(ref, ref, device)

    def push(self):
        self.up_low = self.send(0, self.low, self.axis.up)
        self.down_high = self.send(0, self.high, self.axis.down)
        self.up_high = self.send(0, self.high, self.axis.up)
        self.down_low = self.send(0, self.low, self.axis.down)

    def relay(self):
        self.up_low.wait_recv()
        self.far_low = self.send(3, self.low, self.axis.up)
        self.down_high.wait_recv()
        self.far_high = self.send(1, self.high, self.axis.down)

    def near(self):
        self.up_high.wait_recv()
        self.down_low.wait_recv()

    def far(self):
        self.far_low.wait_recv()
        self.far_high.wait_recv()


class SumAll:
    def __init__(self, links, here, term, result, relay, came, own, got):
        x = here.x
        self.links, self.own, self.got = links, own, got
        self.ring = Sum4(
            links, x, lambda k: term.at[x.at(k)], (relay.at[0], relay.at[1], came.at[0], came.at[1])
        )
        self.share = Share4(links, x, lambda k: result.at[x.at(k)], result.shape[1] // 2)
        self.slot = result.at[x.position]
        pairs = (here.z.pair, here.z.other_pair, here.y.pair, here.y.other_pair, here.sibling)
        self.steps = self.run(pairs)

    def run(self, pairs):
        self.ring.push()
        yield
        self.ring.relay()
        yield
        total = self.ring.finish()
        for at, pair in enumerate(pairs):
            self.own[at] = total
            copy = self.links.start(self.own.at[at], self.got.at[at], pair)
            yield
            copy.wait_recv()
            total = self.own[at] + self.got[at]
        self.slot[...] = total
        self.share.push()
        yield
        self.share.relay()
        yield
        self.share.near()
        self.share.far()

    def next(self):
        next(self.steps, None)


def activation(value):
    root = 0.7978845608028654
    square = value * value
    t = jnp.tanh(root * (value + 0.044715 * (value * square)))
    half = 0.5 * (1.0 + t)
    slope = half + (0.5 * value) * (1.0 - t * t) * (root * (1.0 + 3.0 * 0.044715 * square))
    return value * half, slope


def spread(row):
    wide = jnp.broadcast_to(row, (row.shape[1], row.shape[1]))
    return wide, wide.T


def slot_order(key, source, count, empty):
    lanes = key.shape[1]
    lane = lax.broadcasted_iota(jnp.int32, (lanes, lanes), 1)
    sub = lax.broadcasted_iota(jnp.int32, (lanes, lanes), 0)
    at = lax.broadcasted_iota(jnp.int32, (1, lanes), 1)
    key = jnp.where(at < count, key, 2 * lanes)

    def over(mask, value):
        return jnp.sum(jnp.where(mask, value, 0), axis=0, keepdims=True)

    unique_row, unique_col = spread(key * lanes + at)
    _, rank = spread(over(unique_col < unique_row, 1))
    _, key_col = spread(key)
    _, source_col = spread(source)
    hit = rank == lane
    slot, source, sorted_key = over(hit, sub), over(hit, source_col), over(hit, key_col)
    same = over((rank == lane - 1) & (key_col == sorted_key), 1)
    last = jnp.where(over(key_col == lane, 1) > 0, over(key_col <= lane, 1) - 1, empty)
    return slot, source, same, last


def layer_kernel(
    count_ref, features_ref, weight_ref, adj_ref, rows_ref, cols_ref, cot_ref,
    out_ref, weight_grad_ref, feature_grad_ref,
    x_buf, weight_buf, adj, ids_buf, cot_buf, table_buf, table,
    group_0, group_1, running, parts, relay_buf, from_buf, part2_buf, relay2_buf, from2_buf,
    cot_t, hidden_buf, grad_buf, value_buf, grads_0, grads_1,
    term_buf, term_relay, term_from, term_own, term_got,
    sums, own_buf, twin_buf, relay3_buf, from3_buf, local_sem, send_sem, recv_sem,
):
    here = Place()
    group, grads = (group_0, group_1), (grads_0, grads_1)
    tiles, width, tile = parts.shape[2], parts.shape[3], parts.shape[4]
    slots = adj.shape[0]
    links = Links(send_sem, recv_sem)
    loads = [
        pltpu.make_async_copy(src, dst, local_sem.at[i])
        for i, (src, dst) in enumerate(
            (
                (features_ref, x_buf),
                (rows_ref, ids_buf.at[0]),
                (cols_ref, ids_buf.at[1]),
                (adj_ref, adj),
                (weight_ref, weight_buf),
                (cot_ref, cot_buf),
            )
        )
    ]
    for load in loads:
        load.start()
    met = here.greet()
    feature_halves = node_halves = (0, 1)

    def tile_rows(t):
        return pl.ds(t * tile, tile)

    shares = []
    twins = [[], []]

    def row_slot(h, k):
        return group[h].at[here.y.at(k) * 2 + here.core]

    def across(h, k, rows):
        ref = row_slot(h, k).at[rows]
        twins[h].append(links.start(ref, ref, here.sibling))

    loads[0].wait()
    for h in feature_halves:
        for t in range(tiles):
            block = x_buf[tile_rows(t), pl.ds(h * width, width)]
            group[h][here.row, t] = block.astype(F32).T.astype(BF16)
        if h == 0:
            met()
        share = Share4(links, here.y, lambda k, h=h: row_slot(h, k), tiles // 2)
        share.push()
        low, high = share.low, share.high
        across(h, 0, low)
        across(h, 0, high)
        shares.append(share)

    loads[1].wait()
    loads[2].wait()
    table_buf[...] = jnp.zeros_like(table_buf)
    for i in (0, 1):
        table_buf[i : i + 1, 0:slots] = ids_buf[i]
    by_row, by_col = table_buf[0:1, :], table_buf[1:2, :]
    count = count_ref[0]
    order = slot_order(by_row, by_col, count, slots) + slot_order(by_col, by_row, count, slots)
    for i, line in enumerate(order):
        table_buf[i : i + 1, :] = line
    to_scalars = pltpu.make_async_copy(table_buf, table, local_sem.at[6])
    to_scalars.start()
    running[slots] = jnp.zeros(running.shape[1:], BF16)

    def gather_near(h):
        shares[h].relay()
        across(h, 3, low)
        across(h, 1, high)
        shares[h].near()
        across(h, 3, high)
        across(h, 1, low)

    def gather_far(h):
        shares[h].far()
        across(h, 2, low)
        across(h, 2, high)

    def gather_done(h):
        for copy in twins[h]:
            copy.wait_recv()

    def tile_pass(source, backward):
        base = 4 if backward else 0
        contract = ((1,), (0,)) if backward else ((1,), (1,))

        def step(block, acc):
            products = []
            for k in range(UNROLL):
                at = block * UNROLL + k
                node = table[base + 1, at]
                products.append(
                    lax.dot_general(
                        source[lax.div(node, tiles), lax.rem(node, tiles)],
                        adj[table[base, at]],
                        (contract, ((), ())),
                        preferred_element_type=F32,
                    )
                )
            for k in range(UNROLL):
                at = block * UNROLL + k
                acc = acc * table[base + 2, at].astype(F32) + products[k]
                running[at] = acc.astype(BF16)
            return acc

        lax.fori_loop(0, slots // UNROLL, step, jnp.zeros((width, tile), F32))

    def pick(target, base, block):
        for t in range(tiles):
            target[block, t] = running[table[base + 3, block * tiles + t]]

    firsts, seconds = (here.z, here.x), (here.x, here.z)
    node_slices = [pl.ds(a * (tiles // 2), tiles // 2) for a in node_halves]

    def col_of(a, first, second):
        return second * RING + first if a == 0 else first * RING + second

    def sum_first(h, a, delta):
        first, second = firsts[a], seconds[a]

        def part(k):
            return parts.at[h, col_of(a, first.at(k), second.at(delta)), node_slices[a]]

        r, f = relay_buf.at[h, a, delta], from_buf.at[h, a, delta]
        return Sum4(links, first, part, (r.at[0], r.at[1], f.at[0], f.at[1]))

    def sum_second(h, a):
        r, f = relay2_buf.at[h, a], from2_buf.at[h, a]
        return Sum4(
            links, seconds[a], lambda k: part2_buf.at[h, a, k], (r.at[0], r.at[1], f.at[0], f.at[1])
        )

    first_sums = [
        [[sum_first(h, a, d) for d in range(RING)] for a in node_halves] for h in feature_halves
    ]
    last_sums = [[sum_second(h, a) for a in node_halves] for h in feature_halves]

    def push_first(h, d):
        for a in node_halves:
            first_sums[h][a][d].push()

    def relay_first(h, d):
        for a in node_halves:
            first_sums[h][a][d].relay()

    def done_first(h, a, d):
        part2_buf[h, a, d] = first_sums[h][a][d].finish().astype(BF16)

    def scatter_start(h):
        lax.fori_loop(0, RING * RING, lambda b, _: (pick(parts.at[h], 0, b), 0)[1], 0)
        for d in (2, 1, 3):
            push_first(h, d)

    def scatter_relay(h):
        relay_first(h, 2)
        push_first(h, 0)
        relay_first(h, 1)

    def scatter_far(h):
        for a in node_halves:
            done_first(h, a, 2)
            last_sums[h][a].push_far()
        relay_first(h, 3)
        relay_first(h, 0)

    def scatter_last(h):
        for a in node_halves:
            done_first(h, a, 1)
            last_sums[h][a].push_up()
            done_first(h, a, 3)
            last_sums[h][a].push_down()

    def scatter_end(h):
        for a in node_halves:
            last_sums[h][a].relay()
        for a in node_halves:
            done_first(h, a, 0)

    gather_near(0)
    gather_far(0)
    gather_near(1)
    gather_done(0)
    to_scalars.wait()
    loads[3].wait()
    tile_pass(group[0], False)
    scatter_start(0)
    gather_far(1)
    gather_done(1)
    tile_pass(group[1], False)
    scatter_start(1)
    scatter_relay(0)
    loads[4].wait()
    loads[5].wait()
    for t in range(tiles):
        cot_t[t] = cot_buf[tile_rows(t), :].astype(F32).T
    scatter_relay(1)
    scatter_far(0)
    scatter_far(1)
    scatter_last(0)
    scatter_last(1)
    scatter_end(0)
    scatter_end(1)

    weight = weight_buf[...]

    def dense(a):
        whole = [last_sums[h][a].finish().astype(BF16) for h in feature_halves]
        for i in range(tiles // 2):
            t = a * (tiles // 2) + i
            hidden = jnp.concatenate([whole[0][i], whole[1][i]], axis=0)
            pre_act = lax.dot_general(
                weight, hidden, (((0,), (0,)), ((), ())), preferred_element_type=F32
            )
            value, slope = activation(pre_act)
            pre_grad = (cot_t[t] * slope).astype(BF16)
            own = jnp.dot(weight, pre_grad, preferred_element_type=F32).astype(BF16)
            for h in feature_halves:
                grads[h][here.col, t] = own[h * width : (h + 1) * width]
            value_buf[t] = value
            hidden_buf[t] = hidden
            grad_buf[t] = pre_grad

    def share_first(h, a):
        first, second = seconds[a], firsts[a]
        return Share4(
            links,
            first,
            lambda k: grads[h].at[col_of(1 - a, first.at(k), second.position), node_slices[a]],
            tiles // 4,
        )

    def share_second(h, a, delta):
        first, second = seconds[a], firsts[a]
        return Share4(
            links,
            second,
            lambda k: grads[h].at[col_of(1 - a, first.at(delta), second.at(k)), node_slices[a]],
            tiles // 4,
        )

    ones = [[share_first(h, a) for a in node_halves] for h in feature_halves]
    twos = [
        [[share_second(h, a, d) for a in node_halves] for d in range(RING)] for h in feature_halves
    ]

    def each(things, *verbs):
        for verb in verbs:
            for thing in things:
                getattr(thing, verb)()

    totals = [
        Sum4(
            links,
            here.y,
            lambda k, h=h: own_buf.at[h, k],
            (relay3_buf.at[h, 0], relay3_buf.at[h, 1], from3_buf.at[h, 0], from3_buf.at[h, 1]),
        )
        for h in feature_halves
    ]
    near_order = (2, 1, 3, 0)
    exchanged = [{}, {}]

    def block(h, k, core):
        return sums.at[h, here.y.at(k) * 2 + core]

    def back_start(h):
        tile_pass(grads[h], True)
        lax.fori_loop(0, RING * 2, lambda b, _: (pick(sums.at[h], 4, b), 0)[1], 0)
        for k in near_order:
            exchanged[h][k] = links.start(
                block(h, k, 1 - here.core), twin_buf.at[h, k], here.sibling
            )

    def back_push(h):
        pushes = {2: totals[h].push_far, 1: totals[h].push_up, 3: totals[h].push_down}
        for k in near_order:
            exchanged[h][k].wait_recv()
            own = block(h, k, here.core)[...].astype(F32) + twin_buf[h, k].astype(F32)
            own_buf[h, k] = own.astype(BF16)
            if k in pushes:
                pushes[k]()

    def back_end(h):
        whole = totals[h].finish()
        for t in range(tiles):
            feature_grad_ref[tile_rows(t), pl.ds(h * width, width)] = whole[t].T.astype(BF16)

    for a in node_halves:
        dense(a)
        ones[0][a].push()
        twos[0][0][a].push()
    for t in range(tiles):
        term = lax.dot_general(
            hidden_buf[t], grad_buf[t], (((1,), (1,)), ((), ())), preferred_element_type=F32
        ).reshape(term_buf.shape)
        if t == 0:
            term_buf[...] = term
        else:
            term_buf[...] += term
    weights = SumAll(
        links, here, term_buf, weight_grad_ref, term_relay, term_from, term_own, term_got
    )
    each(ones[0], "relay")
    weights.next()
    each(ones[1], "push")
    each(ones[0], "near")
    each(twos[0][1] + twos[0][3], "push")
    each(twos[0][0], "relay")
    weights.next()
    each(ones[0], "far")
    each(twos[0][2], "push")
    each(twos[1][0], "push")
    weights.next()
    each(ones[1], "relay")
    each(twos[0][1] + twos[0][3], "relay")
    weights.next()
    each(ones[1], "near")
    each(twos[1][1] + twos[1][3], "push")
    each(twos[0][2], "relay")
    weights.next()
    each(twos[1][0], "relay")
    for d in (0, 1, 3, 2):
        each(twos[0][d], "near", "far")
    each(ones[1], "far")
    each(twos[1][2], "push")
    weights.next()
    back_start(0)
    each(twos[1][1] + twos[1][3], "relay")
    weights.next()
    back_push(0)
    each(twos[1][2], "relay")
    weights.next()
    totals[0].relay()
    for t in range(tiles):
        out_ref[tile_rows(t), :] = value_buf[t].T.astype(BF16)
    weights.next()
    for d in (0, 1, 3, 2):
        each(twos[1][d], "near", "far")
    back_start(1)
    weights.next()
    back_push(1)
    back_end(0)
    weights.next()
    totals[1].relay()
    back_end(1)
    links.drain()


def shards(features, weight, adj_tiles, tile_rows, tile_cols, tile_count, cotangent):
    nodes, width = features.shape
    slots, tile = adj_tiles.shape[:2]
    n_row, n_col = lax.axis_size("row"), lax.axis_size("col")
    tiles, half, member = nodes // tile, width // 2, width // RING
    one = (half, tile)

    def vmem(*shape, dtype=BF16):
        return pltpu.VMEM(shape, dtype)

    anywhere = pl.BlockSpec(memory_space=pl.ANY)
    in_vmem = pl.BlockSpec(memory_space=pltpu.VMEM)
    out_features, weight_grad, feature_grad = pl.pallas_call(
        layer_kernel,
        out_shape=(
            jax.ShapeDtypeStruct((nodes, width), BF16),
            jax.ShapeDtypeStruct((RING, member, width), F32),
            jax.ShapeDtypeStruct((nodes, width), BF16),
        ),
        in_specs=[pl.BlockSpec(memory_space=pltpu.SMEM)] + [anywhere] * 6,
        out_specs=(in_vmem,) * 3,
        scratch_shapes=[
            vmem(nodes, width),
            vmem(width, width),
            vmem(slots, tile, tile),
            vmem(2, 1, slots, dtype=jnp.int32),
            vmem(nodes, width),
            vmem(8, 128, dtype=jnp.int32),
            pltpu.SMEM((8, 128), jnp.int32),
            vmem(n_row, tiles, *one),
            vmem(n_row, tiles, *one),
            vmem(slots + 1, *one),
            vmem(2, n_col, tiles, *one),
            vmem(2, 2, RING, 2, tiles // 4, *one),
            vmem(2, 2, RING, 2, tiles // 2, *one),
            vmem(2, 2, RING, tiles // 2, *one),
            vmem(2, 2, 2, tiles // 4, *one),
            vmem(2, 2, 2, tiles // 2, *one),
            vmem(tiles, width, tile, dtype=F32),
            vmem(tiles, width, tile),
            vmem(tiles, width, tile),
            vmem(tiles, width, tile, dtype=F32),
            vmem(n_col, tiles, *one),
            vmem(n_col, tiles, *one),
            vmem(RING, member, width, dtype=F32),
            vmem(2, member // 2, width, dtype=F32),
            vmem(2, member, width, dtype=F32),
            vmem(5, member, width, dtype=F32),
            vmem(5, member, width, dtype=F32),
            vmem(2, n_row, tiles, *one),
            vmem(2, RING, tiles, *one),
            vmem(2, RING, tiles, *one),
            vmem(2, 2, tiles // 2, *one),
            vmem(2, 2, tiles, *one),
            pltpu.SemaphoreType.DMA((7,)),
            pltpu.SemaphoreType.DMA((305,)),
            pltpu.SemaphoreType.DMA((305,)),
        ],
        compiler_params=pltpu.CompilerParams(
            vmem_limit_bytes=VMEM_BYTES, collective_id=0, has_side_effects=True
        ),
        name="layer",
    )(
        tile_count, features, weight, adj_tiles,
        tile_rows.reshape(1, slots), tile_cols.reshape(1, slots), cotangent,
    )
    return (out_features, weight_grad.reshape(width, width), feature_grad)


def solution(mesh):
    in_specs = (
        P(("row", "col"), None),
        P(),
        P(("row", "col"), None, None),
        P(("row", "col")),
        P(("row", "col")),
        P(("row", "col")),
        P(("row", "col"), None),
    )
    out_specs = (P(("row", "col"), None), P(), P(("row", "col"), None))
    return jax.shard_map(shards, mesh=mesh, in_specs=in_specs, out_specs=out_specs, check_vma=False)
```

time: 115 us -> 101 us (0.88)
  Pallas kernels: 105 us -> 94.8 us
  local copies, waits for them, and re-layouts: 8.13 us -> 4.81 us
    pallas_call x5 -> x1, Pallas kernels: 105 us -> 94.8 us  [shards(): pl.pallas_call(layer_kernel, out_shape=(jax.ShapeDtypeStruct((nodes, widt...]
    unnamed x23 -> x3, local copies, waits for them, and re-layouts: 8.13 us -> 4.81 us
where the time goes in v3:
time: 101 us
  Pallas kernels  94.8 us (94%)
  local copies, waits for them, and re-layouts  4.81 us (5%)
  between operations  1.29 us (1%)
    pallas_call x1, Pallas kernels, shards(): pl.pallas_call(layer_kernel, out_shape=(jax.ShapeDtypeStruct((nodes, widt...  94.8 us
    unnamed x3, local copies, waits for them, and re-layouts  4.81 us

profile of v3, /device:TPU:1, one launch (start us, length us, event | category | flops | bytes accessed | tf_op | source)
XLA Modules:
  0.0 100.9 jit_solution(2981154848432348950)
XLA Ops:
  1.3 94.8 %layer.1 = (bf16[1024,128]{1,0:T(8,128)(2,1)}, f32[4,32,128]{2,1,0:T(8,128)}, bf16[1024,128]{1,0:T(8,128)(2,1)}) custom-call(s32[1]{0:T(128)S(6)} %copy.13.count_ref, bf16[1024,128]{1,0:T(8,128)(2,1)} %features_ref.1, bf16[128,128]{1,0:T(8,128)(2,1)} %weight_ref.1, bf16[96,128,128]{2,1,0:T(8,128)(2,1)} %adj_ref.1, s32[1,96]{1,0:T(1,128)} %bitcast.4, ...), custom_call_target="tpu_custom_call" | custom-call | tf_op jit(solution)/shard_map/layer/pallas_call | solution.py:595
  96.0 1.7 %copy.14 = bf16[1024,128]{1,0:T(8,128)(2,1)} copy(bf16[1024,128]{1,0:T(8,128)(2,1)} %get-tuple-element.12) | data formatting | bytes 524288
  97.7 1.5 %copy.15 = f32[128,128]{1,0:T(8,128)} copy(f32[128,128]{1,0:T(8,128)} %bitcast.3) | data formatting | bytes 131072
  99.2 1.7 %copy.16 = bf16[1024,128]{1,0:T(8,128)(2,1)} copy(bf16[1024,128]{1,0:T(8,128)(2,1)} %get-tuple-element.14) | data formatting | bytes 524288

commit v4 on v3

--- a/solution.py
+++ b/solution.py
@@ -14,25 +14,33 @@
 
 class Links:
     def __init__(self, send_sem, recv_sem):
-        self.send_sem, self.recv_sem, self.copies = send_sem, recv_sem, []
-
-    def start(self, src, dst, device):
-        at = len(self.copies)
-        copy = pltpu.make_async_remote_copy(
+        self.send_sem, self.recv_sem = send_sem, recv_sem
+        self.used, self.phases = 0, []
+
+    def semaphore(self):
+        self.used += 1
+        return self.recv_sem.at[self.used - 1]
+
+    def phase(self, ref):
+        self.phases.append(ref)
+        return len(self.phases) - 1
+
+    def start(self, src, dst, device, arrived, phase):
+        pltpu.make_async_remote_copy(
             src_ref=src,
             dst_ref=dst,
-            send_sem=self.send_sem.at[at],
-            recv_sem=self.recv_sem.at[at],
+            send_sem=self.send_sem.at[phase],
+            recv_sem=arrived,
             device_id=device,
             device_id_type=MESH,
-        )
-        copy.start()
-        self.copies.append(copy)
-        return copy
+        ).start()
+
+    def wait(self, arrived, ref):
+        pltpu.make_async_copy(ref, ref, arrived).wait()
 
     def drain(self):
-        for copy in self.copies:
-            copy.wait_send()
+        for at, ref in enumerate(self.phases):
+            self.wait(self.send_sem.at[at], ref)
 
 
 class Axis:
@@ -75,26 +83,29 @@
 
 
 class Sum4:
-    def __init__(self, links, axis, part, buffers):
+    def __init__(self, links, axis, part, relays, blocks, passing, arrived, phase):
         self.links, self.axis, self.part = links, axis, part
-        self.relay_up, self.relay_down, self.from_down, self.from_up = buffers
-        half = self.relay_up.shape[0]
+        self.relay_up, self.relay_down = relays.at[0], relays.at[1]
+        self.from_down, self.from_up = blocks.at[0], blocks.at[1]
+        self.passing, self.arrived, self.phase = passing, arrived, phase
+        half = relays.shape[1]
         self.low, self.high = pl.ds(0, half), pl.ds(half, half)
+
+    def send(self, src, dst, device, arrived):
+        self.links.start(src, dst, device, arrived, self.phase)
 
     def push_far(self):
         far = self.part(2)
-        self.c_up = self.links.start(far.at[self.low], self.relay_up, self.axis.up)
-        self.c_down = self.links.start(far.at[self.high], self.relay_down, self.axis.down)
+        self.send(far.at[self.low], self.relay_up, self.axis.up, self.passing)
+        self.send(far.at[self.high], self.relay_down, self.axis.down, self.passing)
 
     def push_up(self):
-        self.n_up = self.links.start(
-            self.part(1).at[self.high], self.from_down.at[self.high], self.axis.up
-        )
+        near = self.part(1).at[self.high]
+        self.send(near, self.from_down.at[self.high], self.axis.up, self.arrived)
 
     def push_down(self):
-        self.n_down = self.links.start(
-            self.part(3).at[self.low], self.from_up.at[self.low], self.axis.down
-        )
+        near = self.part(3).at[self.low]
+        self.send(near, self.from_up.at[self.low], self.axis.down, self.arrived)
 
     def push(self):
         self.push_far()
@@ -102,20 +113,12 @@
         self.push_down()
 
     def relay(self):
-        self.c_up.wait_recv()
-        mine = self.part(1)[self.low]
-        add_to(self.relay_up, mine)
-        self.r_up = self.links.start(self.relay_up, self.from_down.at[self.low], self.axis.up)
-        self.c_down.wait_recv()
-        mine = self.part(3)[self.high]
-        add_to(self.relay_down, mine)
-        self.r_down = self.links.start(
-            self.relay_down, self.from_up.at[self.high], self.axis.down
-        )
-
-    def finish(self):
-        for copy in (self.n_up, self.n_down, self.r_up, self.r_down):
-            copy.wait_recv()
+        add_to(self.relay_up, self.part(1)[self.low])
+        self.send(self.relay_up, self.from_down.at[self.low], self.axis.up, self.arrived)
+        add_to(self.relay_down, self.part(3)[self.high])
+        self.send(self.relay_down, self.from_up.at[self.high], self.axis.down, self.arrived)
+
+    def total(self):
         return (
             self.part(0)[...].astype(F32)
             + self.from_down[...].astype(F32)
@@ -124,66 +127,65 @@
 
 
 class Share4:
-    def __init__(self, links, axis, slot, half):
+    def __init__(self, links, axis, slot, half, first, near, far, phase):
         self.links, self.axis, self.slot = links, axis, slot
+        self.first, self.near, self.far, self.phase = first, near, far, phase
         self.low, self.high = pl.ds(0, half), pl.ds(half, half)
 
-    def send(self, k, rows, device):
+    def send(self, k, rows, device, arrived):
         ref = self.slot(k).at[rows]
-        return self.links.start(ref, ref, device)
+        self.links.start(ref, ref, device, arrived, self.phase)
 
     def push(self):
-        self.up_low = self.send(0, self.low, self.axis.up)
-        self.down_high = self.send(0, self.high, self.axis.down)
-        self.up_high = self.send(0, self.high, self.axis.up)
-        self.down_low = self.send(0, self.low, self.axis.down)
+        self.send(0, self.low, self.axis.up, self.first)
+        self.send(0, self.high, self.axis.down, self.first)
+        self.send(0, self.high, self.axis.up, self.near)
+        self.send(0, self.low, self.axis.down, self.near)
 
     def relay(self):
-        self.up_low.wait_recv()
-        self.far_low = self.send(3, self.low, self.axis.up)
-        self.down_high.wait_recv()
-        self.far_high = self.send(1, self.high, self.axis.down)
-
-    def near(self):
-        self.up_high.wait_recv()
-        self.down_low.wait_recv()
-
-    def far(self):
-        self.far_low.wait_recv()
-        self.far_high.wait_recv()
+        self.send(3, self.low, self.axis.up, self.far)
+        self.send(1, self.high, self.axis.down, self.far)
 
 
 class SumAll:
     def __init__(self, links, here, term, result, relay, came, own, got):
         x = here.x
-        self.links, self.own, self.got = links, own, got
-        self.ring = Sum4(
-            links, x, lambda k: term.at[x.at(k)], (relay.at[0], relay.at[1], came.at[0], came.at[1])
-        )
-        self.share = Share4(links, x, lambda k: result.at[x.at(k)], result.shape[1] // 2)
+        self.links, self.own, self.got, self.relays, self.came = links, own, got, relay, came
+        self.result = result
+        phase = links.phase(own)
+        passing, arrived, self.first, self.rest = (links.semaphore() for _ in range(4))
+        self.ring = Sum4(links, x, lambda k: term.at[x.at(k)], relay, came, passing, arrived, phase)
+        self.share = Share4(
+            links, x, lambda k: result.at[x.at(k)], result.shape[1] // 2,
+            self.first, self.rest, self.rest, phase,
+        )
         self.slot = result.at[x.position]
         pairs = (here.z.pair, here.z.other_pair, here.y.pair, here.y.other_pair, here.sibling)
         self.steps = self.run(pairs)
 
     def run(self, pairs):
-        self.ring.push()
+        links, ring, share = self.links, self.ring, self.share
+        ring.push()
         yield
-        self.ring.relay()
+        links.wait(ring.passing, self.relays)
+        ring.relay()
         yield
-        total = self.ring.finish()
+        links.wait(ring.arrived, self.came)
+        total = ring.total()
         for at, pair in enumerate(pairs):
             self.own[at] = total
-            copy = self.links.start(self.own.at[at], self.got.at[at], pair)
+            arrived = links.semaphore()
+            links.start(self.own.at[at], self.got.at[at], pair, arrived, ring.phase)
             yield
-            copy.wait_recv()
+            links.wait(arrived, self.got.at[at])
             total = self.own[at] + self.got[at]
         self.slot[...] = total
-        self.share.push()
+        share.push()
         yield
-        self.share.relay()
+        links.wait(self.first, self.result.at[0])
+        share.relay()
         yield
-        self.share.near()
-        self.share.far()
+        links.wait(self.rest, self.result.at[pl.ds(0, 2)])
 
     def next(self):
         next(self.steps, None)
@@ -259,29 +261,58 @@
     def tile_rows(t):
         return pl.ds(t * tile, tile)
 
-    shares = []
-    twins = [[], []]
-
     def row_slot(h, k):
         return group[h].at[here.y.at(k) * 2 + here.core]
 
+    def share_row(h):
+        first, near, far = (links.semaphore() for _ in range(3))
+        phase = links.phase(parts.at[h, pl.ds(0, 7)])
+        return Share4(
+            links, here.y, lambda k: row_slot(h, k), tiles // 2, first, near, far, phase
+        )
+
+    shares = [share_row(h) for h in feature_halves]
+    twins = [links.semaphore() for _ in feature_halves]
+    low, high = shares[0].low, shares[0].high
+
     def across(h, k, rows):
         ref = row_slot(h, k).at[rows]
-        twins[h].append(links.start(ref, ref, here.sibling))
-
-    loads[0].wait()
-    for h in feature_halves:
+        links.start(ref, ref, here.sibling, twins[h], shares[h].phase)
+
+    def gather_load(h):
         for t in range(tiles):
             block = x_buf[tile_rows(t), pl.ds(h * width, width)]
             group[h][here.row, t] = block.astype(F32).T.astype(BF16)
-        if h == 0:
-            met()
-        share = Share4(links, here.y, lambda k, h=h: row_slot(h, k), tiles // 2)
-        share.push()
-        low, high = share.low, share.high
+
+    def gather_push(h):
+        shares[h].push()
         across(h, 0, low)
         across(h, 0, high)
-        shares.append(share)
+
+    def gather_relay(h):
+        links.wait(shares[h].first, group[h].at[0])
+        shares[h].relay()
+        across(h, 3, low)
+        across(h, 1, high)
+
+    def gather_near(h):
+        links.wait(shares[h].near, group[h].at[0])
+        across(h, 3, high)
+        across(h, 1, low)
+
+    def gather_far(h):
+        links.wait(shares[h].far, group[h].at[0])
+        across(h, 2, low)
+        across(h, 2, high)
+
+    def gather_done(h):
+        links.wait(twins[h], group[h].at[pl.ds(0, 4)])
+
+    loads[0].wait()
+    gather_load(0)
+    met()
+    gather_push(0)
+    gather_load(1)
 
     loads[1].wait()
     loads[2].wait()
@@ -296,23 +327,6 @@
     to_scalars = pltpu.make_async_copy(table_buf, table, local_sem.at[6])
     to_scalars.start()
     running[slots] = jnp.zeros(running.shape[1:], BF16)
-
-    def gather_near(h):
-        shares[h].relay()
-        across(h, 3, low)
-        across(h, 1, high)
-        shares[h].near()
-        across(h, 3, high)
-        across(h, 1, low)
-
-    def gather_far(h):
-        shares[h].far()
-        across(h, 2, low)
-        across(h, 2, high)
-
-    def gather_done(h):
-        for copy in twins[h]:
-            copy.wait_recv()
 
     def tile_pass(source, backward):
         base = 4 if backward else 0
@@ -349,19 +363,27 @@
     def col_of(a, first, second):
         return second * RING + first if a == 0 else first * RING + second
 
+    passing, arrived = (
+        [[links.semaphore() for _ in range(RING)] for _ in feature_halves] for _ in range(2)
+    )
+    passing_2, arrived_2 = ([links.semaphore() for _ in feature_halves] for _ in range(2))
+    phases = [links.phase(parts.at[h, pl.ds(0, 15)]) for h in feature_halves]
+
     def sum_first(h, a, delta):
         first, second = firsts[a], seconds[a]
 
         def part(k):
             return parts.at[h, col_of(a, first.at(k), second.at(delta)), node_slices[a]]
 
-        r, f = relay_buf.at[h, a, delta], from_buf.at[h, a, delta]
-        return Sum4(links, first, part, (r.at[0], r.at[1], f.at[0], f.at[1]))
+        return Sum4(
+            links, first, part, relay_buf.at[h, delta, a], from_buf.at[h, delta, a],
+            passing[h][delta], arrived[h][delta], phases[h],
+        )
 
     def sum_second(h, a):
-        r, f = relay2_buf.at[h, a], from2_buf.at[h, a]
         return Sum4(
-            links, seconds[a], lambda k: part2_buf.at[h, a, k], (r.at[0], r.at[1], f.at[0], f.at[1])
+            links, seconds[a], lambda k: part2_buf.at[h, a, k], relay2_buf.at[h, a],
+            from2_buf.at[h, a], passing_2[h], arrived_2[h], phases[h],
         )
 
     first_sums = [
@@ -374,50 +396,60 @@
             first_sums[h][a][d].push()
 
     def relay_first(h, d):
+        links.wait(passing[h][d], relay_buf.at[h, d])
         for a in node_halves:
             first_sums[h][a][d].relay()
 
+    def wait_first(h, d):
+        links.wait(arrived[h][d], from_buf.at[h, d])
+
     def done_first(h, a, d):
-        part2_buf[h, a, d] = first_sums[h][a][d].finish().astype(BF16)
+        part2_buf[h, a, d] = first_sums[h][a][d].total().astype(BF16)
 
     def scatter_start(h):
         lax.fori_loop(0, RING * RING, lambda b, _: (pick(parts.at[h], 0, b), 0)[1], 0)
-        for d in (2, 1, 3):
+        for d in (2, 1, 3, 0):
             push_first(h, d)
 
     def scatter_relay(h):
-        relay_first(h, 2)
-        push_first(h, 0)
-        relay_first(h, 1)
+        for d in (2, 1, 3, 0):
+            relay_first(h, d)
 
     def scatter_far(h):
+        wait_first(h, 2)
         for a in node_halves:
             done_first(h, a, 2)
             last_sums[h][a].push_far()
-        relay_first(h, 3)
-        relay_first(h, 0)
-
-    def scatter_last(h):
+
+    def scatter_near(h):
+        wait_first(h, 1)
         for a in node_halves:
             done_first(h, a, 1)
             last_sums[h][a].push_up()
+        wait_first(h, 3)
+        for a in node_halves:
             done_first(h, a, 3)
             last_sums[h][a].push_down()
 
     def scatter_end(h):
+        links.wait(passing_2[h], relay2_buf.at[h])
         for a in node_halves:
             last_sums[h][a].relay()
+        wait_first(h, 0)
         for a in node_halves:
             done_first(h, a, 0)
 
+    gather_relay(0)
+    gather_push(1)
     gather_near(0)
     gather_far(0)
-    gather_near(1)
+    gather_relay(1)
     gather_done(0)
     to_scalars.wait()
     loads[3].wait()
     tile_pass(group[0], False)
     scatter_start(0)
+    gather_near(1)
     gather_far(1)
     gather_done(1)
     tile_pass(group[1], False)
@@ -430,15 +462,15 @@
     scatter_relay(1)
     scatter_far(0)
     scatter_far(1)
-    scatter_last(0)
-    scatter_last(1)
+    scatter_near(0)
+    scatter_near(1)
     scatter_end(0)
     scatter_end(1)
 
     weight = weight_buf[...]
 
     def dense(a):
-        whole = [last_sums[h][a].finish().astype(BF16) for h in feature_halves]
+        whole = [last_sums[h][a].total().astype(BF16) for h in feature_halves]
         for i in range(tiles // 2):
             t = a * (tiles // 2) + i
             hidden = jnp.concatenate([whole[0][i], whole[1][i]], axis=0)
@@ -454,6 +486,11 @@
             hidden_buf[t] = hidden
             grad_buf[t] = pre_grad
 
+    share_phases = [links.phase(parts.at[h, pl.ds(0, 15)]) for h in feature_halves]
+    one_sems = [[links.semaphore() for _ in range(3)] for _ in feature_halves]
+    two_sems = [[links.semaphore() for _ in range(RING)] for _ in feature_halves]
+    rest_sems = [links.semaphore() for _ in feature_halves]
+
     def share_first(h, a):
         first, second = seconds[a], firsts[a]
         return Share4(
@@ -461,6 +498,8 @@
             first,
             lambda k: grads[h].at[col_of(1 - a, first.at(k), second.position), node_slices[a]],
             tiles // 4,
+            *one_sems[h],
+            share_phases[h],
         )
 
     def share_second(h, a, delta):
@@ -470,6 +509,10 @@
             second,
             lambda k: grads[h].at[col_of(1 - a, first.at(delta), second.at(k)), node_slices[a]],
             tiles // 4,
+            two_sems[h][delta],
+            rest_sems[h],
+            rest_sems[h],
+            share_phases[h],
         )
 
     ones = [[share_first(h, a) for a in node_halves] for h in feature_halves]
@@ -477,48 +520,76 @@
         [[share_second(h, a, d) for a in node_halves] for d in range(RING)] for h in feature_halves
     ]
 
-    def each(things, *verbs):
-        for verb in verbs:
-            for thing in things:
-                getattr(thing, verb)()
-
+    def one_push(h):
+        for share in ones[h]:
+            share.push()
+
+    def one_wait(h, which):
+        links.wait(one_sems[h][which], grads[h].at[0])
+
+    def one_relay(h):
+        one_wait(h, 0)
+        for share in ones[h]:
+            share.relay()
+
+    def two_push(h, *offsets):
+        for d in offsets:
+            for share in twos[h][d]:
+                share.push()
+
+    def two_relay(h, *offsets):
+        for d in offsets:
+            links.wait(two_sems[h][d], grads[h].at[0])
+            for share in twos[h][d]:
+                share.relay()
+
+    def shared(h):
+        links.wait(rest_sems[h], grads[h].at[pl.ds(0, 8)])
+
+    back_phases = [links.phase(parts.at[h, pl.ds(0, 7)]) for h in feature_halves]
+    passing_3, arrived_3 = ([links.semaphore() for _ in feature_halves] for _ in range(2))
+    swapped = [[links.semaphore() for _ in range(RING)] for _ in feature_halves]
     totals = [
         Sum4(
-            links,
-            here.y,
-            lambda k, h=h: own_buf.at[h, k],
-            (relay3_buf.at[h, 0], relay3_buf.at[h, 1], from3_buf.at[h, 0], from3_buf.at[h, 1]),
+            links, here.y, lambda k, h=h: own_buf.at[h, k], relay3_buf.at[h], from3_buf.at[h],
+            passing_3[h], arrived_3[h], back_phases[h],
         )
         for h in feature_halves
     ]
     near_order = (2, 1, 3, 0)
-    exchanged = [{}, {}]
 
     def block(h, k, core):
         return sums.at[h, here.y.at(k) * 2 + core]
 
-    def back_start(h):
-        tile_pass(grads[h], True)
+    def back_swap(h):
         lax.fori_loop(0, RING * 2, lambda b, _: (pick(sums.at[h], 4, b), 0)[1], 0)
         for k in near_order:
-            exchanged[h][k] = links.start(
-                block(h, k, 1 - here.core), twin_buf.at[h, k], here.sibling
+            links.start(
+                block(h, k, 1 - here.core), twin_buf.at[h, k], here.sibling, swapped[h][k],
+                back_phases[h],
             )
 
     def back_push(h):
         pushes = {2: totals[h].push_far, 1: totals[h].push_up, 3: totals[h].push_down}
         for k in near_order:
-            exchanged[h][k].wait_recv()
+            links.wait(swapped[h][k], twin_buf.at[h, k])
             own = block(h, k, here.core)[...].astype(F32) + twin_buf[h, k].astype(F32)
             own_buf[h, k] = own.astype(BF16)
             if k in pushes:
                 pushes[k]()
 
+    def back_relay(h):
+        links.wait(passing_3[h], relay3_buf.at[h])
+        totals[h].relay()
+
     def back_end(h):
-        whole = totals[h].finish()
+        links.wait(arrived_3[h], from3_buf.at[h])
+        whole = totals[h].total()
         for t in range(tiles):
             feature_grad_ref[tile_rows(t), pl.ds(h * width, width)] = whole[t].T.astype(BF16)
 
+    for h in feature_halves:
+        links.wait(arrived_2[h], from2_buf.at[h])
     for a in node_halves:
         dense(a)
         ones[0][a].push()
@@ -534,50 +605,62 @@
     weights = SumAll(
         links, here, term_buf, weight_grad_ref, term_relay, term_from, term_own, term_got
     )
-    each(ones[0], "relay")
-    weights.next()
-    each(ones[1], "push")
-    each(ones[0], "near")
-    each(twos[0][1] + twos[0][3], "push")
-    each(twos[0][0], "relay")
-    weights.next()
-    each(ones[0], "far")
-    each(twos[0][2], "push")
-    each(twos[1][0], "push")
-    weights.next()
-    each(ones[1], "relay")
-    each(twos[0][1] + twos[0][3], "relay")
-    weights.next()
-    each(ones[1], "near")
-    each(twos[1][1] + twos[1][3], "push")
-    each(twos[0][2], "relay")
-    weights.next()
-    each(twos[1][0], "relay")
-    for d in (0, 1, 3, 2):
-        each(twos[0][d], "near", "far")
-    each(ones[1], "far")
-    each(twos[1][2], "push")
-    weights.next()
-    back_start(0)
-    each(twos[1][1] + twos[1][3], "relay")
+    one_relay(0)
+    one_wait(0, 1)
+    two_push(0, 1, 3)
+    weights.next()
+    two_relay(0, 0)
+    one_wait(0, 2)
+    two_push(0, 2)
+    two_relay(0, 1)
+    weights.next()
+    two_relay(0, 3)
+    two_relay(0, 2)
+    one_push(1)
+    two_push(1, 0)
+    weights.next()
+    shared(0)
+    tile_pass(grads[0], True)
+    one_relay(1)
+    one_wait(1, 1)
+    two_push(1, 1, 3)
+    weights.next()
+    two_relay(1, 0)
+    back_swap(0)
+    one_wait(1, 2)
+    two_push(1, 2)
     weights.next()
     back_push(0)
-    each(twos[1][2], "relay")
-    weights.next()
-    totals[0].relay()
+    two_relay(1, 1)
+    two_relay(1, 3)
+    weights.next()
+    back_relay(0)
+    two_relay(1, 2)
+    weights.next()
     for t in range(tiles):
         out_ref[tile_rows(t), :] = value_buf[t].T.astype(BF16)
     weights.next()
-    for d in (0, 1, 3, 2):
-        each(twos[1][d], "near", "far")
-    back_start(1)
+    back_end(0)
+    shared(1)
+    tile_pass(grads[1], True)
+    back_swap(1)
     weights.next()
     back_push(1)
-    back_end(0)
-    weights.next()
-    totals[1].relay()
+    weights.next()
+    back_relay(1)
     back_end(1)
     links.drain()
+
+
+def copy_kernel(*refs):
+    half = len(refs) // 2
+    copies = [
+        pltpu.make_async_copy(refs[i], refs[half + i], refs[-1].at[i]) for i in range(half)
+    ]
+    for copy in copies:
+        copy.start()
+    for copy in copies:
+        copy.wait()
 
 
 def shards(features, weight, adj_tiles, tile_rows, tile_cols, tile_count, cotangent):
@@ -592,7 +675,7 @@
 
     anywhere = pl.BlockSpec(memory_space=pl.ANY)
     in_vmem = pl.BlockSpec(memory_space=pltpu.VMEM)
-    out_features, weight_grad, feature_grad = pl.pallas_call(
+    results = pl.pallas_call(
         layer_kernel,
         out_shape=(
             jax.ShapeDtypeStruct((nodes, width), BF16),
@@ -613,8 +696,8 @@
             vmem(n_row, tiles, *one),
             vmem(slots + 1, *one),
             vmem(2, n_col, tiles, *one),
-            vmem(2, 2, RING, 2, tiles // 4, *one),
-            vmem(2, 2, RING, 2, tiles // 2, *one),
+            vmem(2, RING, 2, 2, tiles // 4, *one),
+            vmem(2, RING, 2, 2, tiles // 2, *one),
             vmem(2, 2, RING, tiles // 2, *one),
             vmem(2, 2, 2, tiles // 4, *one),
             vmem(2, 2, 2, tiles // 2, *one),
@@ -627,7 +710,7 @@
             vmem(RING, member, width, dtype=F32),
             vmem(2, member // 2, width, dtype=F32),
             vmem(2, member, width, dtype=F32),
-            vmem(5, member, width, dtype=F32),
+            vmem(11, member, width, dtype=F32),
             vmem(5, member, width, dtype=F32),
             vmem(2, n_row, tiles, *one),
             vmem(2, RING, tiles, *one),
@@ -635,8 +718,8 @@
             vmem(2, 2, tiles // 2, *one),
             vmem(2, 2, tiles, *one),
             pltpu.SemaphoreType.DMA((7,)),
-            pltpu.SemaphoreType.DMA((305,)),
-            pltpu.SemaphoreType.DMA((305,)),
+            pltpu.SemaphoreType.DMA((9,)),
+            pltpu.SemaphoreType.DMA((65,)),
         ],
         compiler_params=pltpu.CompilerParams(
             vmem_limit_bytes=VMEM_BYTES, collective_id=0, has_side_effects=True
@@ -646,6 +729,14 @@
         tile_count, features, weight, adj_tiles,
         tile_rows.reshape(1, slots), tile_cols.reshape(1, slots), cotangent,
     )
+    out_features, weight_grad, feature_grad = pl.pallas_call(
+        copy_kernel,
+        out_shape=tuple(jax.ShapeDtypeStruct(r.shape, r.dtype) for r in results),
+        in_specs=[anywhere] * 3,
+        out_specs=(anywhere,) * 3,
+        scratch_shapes=[pltpu.SemaphoreType.DMA((3,))],
+        name="results",
+    )(*results)
     return (out_features, weight_grad.reshape(width, width), feature_grad)
 
 

time: 101 us -> 111 us (1.099)
  Pallas kernels: 94.8 us -> 110 us
  local copies, waits for them, and re-layouts: 4.81 us -> 0 us
    pallas_call x0 -> x1, Pallas kernels: none -> 19 us  [shards(): pl.pallas_call(copy_kernel, out_shape=tuple((jax.ShapeDtypeStruct(r.shape...]
    unnamed x3 -> x0, local copies, waits for them, and re-layouts: 4.81 us -> none
    pallas_call x1, Pallas kernels: 94.8 us -> 90.6 us  [shards(): pl.pallas_call(layer_kernel, out_shape=(jax.ShapeDtypeStruct((nodes, widt...]
where the time goes in v4:
time: 111 us
  Pallas kernels  110 us (99%)
  between operations  1.29 us (1%)
    pallas_call x1, Pallas kernels, shards(): pl.pallas_call(layer_kernel, out_shape=(jax.ShapeDtypeStruct((nodes, widt...  90.6 us
    pallas_call x1, Pallas kernels, shards(): pl.pallas_call(copy_kernel, out_shape=tuple((jax.ShapeDtypeStruct(r.shape...  19 us

profile of v4, /device:TPU:1, one launch (start us, length us, event | category | flops | bytes accessed | tf_op | source)
XLA Modules:
  0.0 110.8 jit_solution(17541885875489137489)
XLA Ops:
  1.3 90.6 %layer.1 = (bf16[1024,128]{1,0:T(8,128)(2,1)}, f32[4,32,128]{2,1,0:T(8,128)}, bf16[1024,128]{1,0:T(8,128)(2,1)}) custom-call(s32[1]{0:T(128)S(6)} %copy.10.count_ref, bf16[1024,128]{1,0:T(8,128)(2,1)} %features_ref.1, bf16[128,128]{1,0:T(8,128)(2,1)} %weight_ref.1, bf16[96,128,128]{2,1,0:T(8,128)(2,1)} %adj_ref.1, s32[1,96]{1,0:T(1,128)} %bitcast.3, ...), custom_call_target="tpu_custom_call" | custom-call | tf_op jit(solution)/shard_map/layer/pallas_call | solution.py:678
  91.8 19.0 %results.1 = (bf16[1024,128]{1,0:T(8,128)(2,1)}, f32[4,32,128]{2,1,0:T(8,128)}, bf16[1024,128]{1,0:T(8,128)(2,1)}) custom-call(bf16[1024,128]{1,0:T(8,128)(2,1)} %get-tuple-element.9.refs_0_, f32[4,32,128]{2,1,0:T(8,128)} %get-tuple-element.10.refs_1_, bf16[1024,128]{1,0:T(8,128)(2,1)} %get-tuple-element.11.refs_2_), custom_call_target="tpu_custom_call" | custom-call | tf_op jit(solution)/shard_map/results/pallas_call | solution.py:732

commit v5 on v4

--- a/solution.py
+++ b/solution.py
@@ -653,13 +653,17 @@
 
 
 def copy_kernel(*refs):
-    half = len(refs) // 2
-    copies = [
-        pltpu.make_async_copy(refs[i], refs[half + i], refs[-1].at[i]) for i in range(half)
-    ]
-    for copy in copies:
+    count = (len(refs) - 2) // 3
+    sources, targets, held = (refs[i * count : (i + 1) * count] for i in range(3))
+    came, left = refs[-2:]
+    into = [pltpu.make_async_copy(sources[i], held[i], came.at[i]) for i in range(count)]
+    out = [pltpu.make_async_copy(held[i], targets[i], left.at[i]) for i in range(count)]
+    for copy in into:
         copy.start()
-    for copy in copies:
+    for first, second in zip(into, out):
+        first.wait()
+        second.start()
+    for copy in out:
         copy.wait()
 
 
@@ -734,7 +738,9 @@
         out_shape=tuple(jax.ShapeDtypeStruct(r.shape, r.dtype) for r in results),
         in_specs=[anywhere] * 3,
         out_specs=(anywhere,) * 3,
-        scratch_shapes=[pltpu.SemaphoreType.DMA((3,))],
+        scratch_shapes=[pltpu.VMEM(r.shape, r.dtype) for r in results]
+        + [pltpu.SemaphoreType.DMA((3,))] * 2,
+        compiler_params=pltpu.CompilerParams(vmem_limit_bytes=VMEM_BYTES),
         name="results",
     )(*results)
     return (out_features, weight_grad.reshape(width, width), feature_grad)

time: 111 us -> 93.8 us (0.85)
  Pallas kernels: 110 us -> 92.4 us
    pallas_call x1, Pallas kernels: 19 us -> 1.82 us  [shards(): pl.pallas_call(copy_kernel, out_shape=tuple((jax.ShapeDtypeStruct(r.shape...]
where the time goes in v5:
time: 93.8 us; the launch traced here: 93.7 us
  Pallas kernels  92.4 us (99%)
  between operations  1.29 us (1%)
    pallas_call x1, Pallas kernels, shards(): pl.pallas_call(layer_kernel, out_shape=(jax.ShapeDtypeStruct((nodes, widt...  90.6 us

profile of v5, /device:TPU:1, one launch (start us, length us, event | category | flops | bytes accessed | tf_op | source)
XLA Modules:
  0.0 93.7 jit_solution(17892527835531911153)
XLA Ops:
  1.3 90.6 %layer.1 = (bf16[1024,128]{1,0:T(8,128)(2,1)}, f32[4,32,128]{2,1,0:T(8,128)}, bf16[1024,128]{1,0:T(8,128)(2,1)}) custom-call(s32[1]{0:T(128)S(6)} %copy.10.count_ref, bf16[1024,128]{1,0:T(8,128)(2,1)} %features_ref.1, bf16[128,128]{1,0:T(8,128)(2,1)} %weight_ref.1, bf16[96,128,128]{2,1,0:T(8,128)(2,1)} %adj_ref.1, s32[1,96]{1,0:T(1,128)} %bitcast.3, ...), custom_call_target="tpu_custom_call" | custom-call | tf_op jit(solution)/shard_map/layer/pallas_call | solution.py:682
  91.8 1.8 %results.1 = (bf16[1024,128]{1,0:T(8,128)(2,1)}, f32[4,32,128]{2,1,0:T(8,128)}, bf16[1024,128]{1,0:T(8,128)(2,1)}) custom-call(bf16[1024,128]{1,0:T(8,128)(2,1)} %get-tuple-element.9.refs_0_, f32[4,32,128]{2,1,0:T(8,128)} %get-tuple-element.10.refs_1_, bf16[1024,128]{1,0:T(8,128)(2,1)} %get-tuple-element.11.refs_2_), custom_call_target="tpu_custom_call" | custom-call | tf_op jit(solution)/shard_map/results/pallas_call | solution.py:736

commit v6 on v5

--- a/solution.py
+++ b/solution.py
@@ -149,18 +149,18 @@
 
 class SumAll:
     def __init__(self, links, here, term, result, relay, came, own, got):
-        x = here.x
+        y = here.y
         self.links, self.own, self.got, self.relays, self.came = links, own, got, relay, came
         self.result = result
         phase = links.phase(own)
         passing, arrived, self.first, self.rest = (links.semaphore() for _ in range(4))
-        self.ring = Sum4(links, x, lambda k: term.at[x.at(k)], relay, came, passing, arrived, phase)
+        self.ring = Sum4(links, y, lambda k: term.at[y.at(k)], relay, came, passing, arrived, phase)
         self.share = Share4(
-            links, x, lambda k: result.at[x.at(k)], result.shape[1] // 2,
+            links, y, lambda k: result.at[y.at(k)], result.shape[1] // 2,
             self.first, self.rest, self.rest, phase,
         )
-        self.slot = result.at[x.position]
-        pairs = (here.z.pair, here.z.other_pair, here.y.pair, here.y.other_pair, here.sibling)
+        self.slot = result.at[y.position]
+        pairs = (here.sibling, here.x.pair, here.z.pair, here.x.other_pair, here.z.other_pair)
         self.steps = self.run(pairs)
 
     def run(self, pairs):
@@ -233,7 +233,8 @@
     group_0, group_1, running, parts, relay_buf, from_buf, part2_buf, relay2_buf, from2_buf,
     cot_t, hidden_buf, grad_buf, value_buf, grads_0, grads_1,
     term_buf, term_relay, term_from, term_own, term_got,
-    sums, own_buf, twin_buf, relay3_buf, from3_buf, local_sem, send_sem, recv_sem,
+    sums, own_buf, twin_buf, relay3_buf, from3_buf,
+    out_buf, weight_grad, feature_grad, count_buf, local_sem, send_sem, recv_sem,
 ):
     here = Place()
     group, grads = (group_0, group_1), (grads_0, grads_1)
@@ -250,6 +251,7 @@
                 (adj_ref, adj),
                 (weight_ref, weight_buf),
                 (cot_ref, cot_buf),
+                (count_ref, count_buf),
             )
         )
     ]
@@ -320,11 +322,12 @@
     for i in (0, 1):
         table_buf[i : i + 1, 0:slots] = ids_buf[i]
     by_row, by_col = table_buf[0:1, :], table_buf[1:2, :]
-    count = count_ref[0]
+    loads[6].wait()
+    count = count_buf[0]
     order = slot_order(by_row, by_col, count, slots) + slot_order(by_col, by_row, count, slots)
     for i, line in enumerate(order):
         table_buf[i : i + 1, :] = line
-    to_scalars = pltpu.make_async_copy(table_buf, table, local_sem.at[6])
+    to_scalars = pltpu.make_async_copy(table_buf, table, local_sem.at[7])
     to_scalars.start()
     running[slots] = jnp.zeros(running.shape[1:], BF16)
 
@@ -354,8 +357,9 @@
         lax.fori_loop(0, slots // UNROLL, step, jnp.zeros((width, tile), F32))
 
     def pick(target, base, block):
+        picked = [running[table[base + 3, block * tiles + t]] for t in range(tiles)]
         for t in range(tiles):
-            target[block, t] = running[table[base + 3, block * tiles + t]]
+            target[block, t] = picked[t]
 
     firsts, seconds = (here.z, here.x), (here.x, here.z)
     node_slices = [pl.ds(a * (tiles // 2), tiles // 2) for a in node_halves]
@@ -562,12 +566,14 @@
         return sums.at[h, here.y.at(k) * 2 + core]
 
     def back_swap(h):
-        lax.fori_loop(0, RING * 2, lambda b, _: (pick(sums.at[h], 4, b), 0)[1], 0)
         for k in near_order:
+            pick(sums.at[h], 4, here.y.at(k) * 2 + 1 - here.core)
             links.start(
                 block(h, k, 1 - here.core), twin_buf.at[h, k], here.sibling, swapped[h][k],
                 back_phases[h],
             )
+        for k in near_order:
+            pick(sums.at[h], 4, here.y.at(k) * 2 + here.core)
 
     def back_push(h):
         pushes = {2: totals[h].push_far, 1: totals[h].push_up, 3: totals[h].push_down}
@@ -586,7 +592,7 @@
         links.wait(arrived_3[h], from3_buf.at[h])
         whole = totals[h].total()
         for t in range(tiles):
-            feature_grad_ref[tile_rows(t), pl.ds(h * width, width)] = whole[t].T.astype(BF16)
+            feature_grad[tile_rows(t), pl.ds(h * width, width)] = whole[t].T.astype(BF16)
 
     for h in feature_halves:
         links.wait(arrived_2[h], from2_buf.at[h])
@@ -602,54 +608,64 @@
             term_buf[...] = term
         else:
             term_buf[...] += term
+    stores = [
+        pltpu.make_async_copy(src, dst, local_sem.at[8 + i])
+        for i, (src, dst) in enumerate(
+            ((out_buf, out_ref), (weight_grad, weight_grad_ref), (feature_grad, feature_grad_ref))
+        )
+    ]
     weights = SumAll(
-        links, here, term_buf, weight_grad_ref, term_relay, term_from, term_own, term_got
+        links, here, term_buf, weight_grad, term_relay, term_from, term_own, term_got
     )
+    weights.next()
     one_relay(0)
     one_wait(0, 1)
     two_push(0, 1, 3)
     weights.next()
+    one_push(1)
     two_relay(0, 0)
+    weights.next()
     one_wait(0, 2)
     two_push(0, 2)
-    two_relay(0, 1)
-    weights.next()
-    two_relay(0, 3)
+    two_push(1, 0)
+    weights.next()
+    two_relay(0, 1, 3)
+    one_relay(1)
+    weights.next()
     two_relay(0, 2)
-    one_push(1)
-    two_push(1, 0)
+    one_wait(1, 1)
+    two_push(1, 1, 3)
+    two_relay(1, 0)
+    one_wait(1, 2)
+    two_push(1, 2)
     weights.next()
     shared(0)
     tile_pass(grads[0], True)
-    one_relay(1)
-    one_wait(1, 1)
-    two_push(1, 1, 3)
-    weights.next()
-    two_relay(1, 0)
     back_swap(0)
-    one_wait(1, 2)
-    two_push(1, 2)
+    two_relay(1, 1, 3)
     weights.next()
     back_push(0)
-    two_relay(1, 1)
-    two_relay(1, 3)
-    weights.next()
-    back_relay(0)
     two_relay(1, 2)
-    weights.next()
-    for t in range(tiles):
-        out_ref[tile_rows(t), :] = value_buf[t].T.astype(BF16)
-    weights.next()
-    back_end(0)
     shared(1)
     tile_pass(grads[1], True)
     back_swap(1)
+    back_relay(0)
     weights.next()
     back_push(1)
     weights.next()
+    for t in range(tiles):
+        out_buf[tile_rows(t), :] = value_buf[t].T.astype(BF16)
+    stores[0].start()
+    back_end(0)
+    weights.next()
     back_relay(1)
+    weights.next()
+    stores[1].start()
     back_end(1)
+    stores[2].start()
     links.drain()
+    for store in stores:
+        store.wait()
 
 
 def copy_kernel(*refs):
@@ -678,7 +694,6 @@
         return pltpu.VMEM(shape, dtype)
 
     anywhere = pl.BlockSpec(memory_space=pl.ANY)
-    in_vmem = pl.BlockSpec(memory_space=pltpu.VMEM)
     results = pl.pallas_call(
         layer_kernel,
         out_shape=(
@@ -686,8 +701,8 @@
             jax.ShapeDtypeStruct((RING, member, width), F32),
             jax.ShapeDtypeStruct((nodes, width), BF16),
         ),
-        in_specs=[pl.BlockSpec(memory_space=pltpu.SMEM)] + [anywhere] * 6,
-        out_specs=(in_vmem,) * 3,
+        in_specs=[anywhere] * 7,
+        out_specs=(anywhere,) * 3,
         scratch_shapes=[
             vmem(nodes, width),
             vmem(width, width),
@@ -721,7 +736,11 @@
             vmem(2, RING, tiles, *one),
             vmem(2, 2, tiles // 2, *one),
             vmem(2, 2, tiles, *one),
-            pltpu.SemaphoreType.DMA((7,)),
+            vmem(nodes, width),
+            vmem(RING, member, width, dtype=F32),
+            vmem(nodes, width),
+            pltpu.SMEM((1,), jnp.int32),
+            pltpu.SemaphoreType.DMA((11,)),
             pltpu.SemaphoreType.DMA((9,)),
             pltpu.SemaphoreType.DMA((65,)),
         ],

time: 93.8 us -> 90 us (0.959)
  Pallas kernels: 92.4 us -> 87.7 us
    pallas_call x1, Pallas kernels: 90.6 us -> 85.8 us  [shards(): pl.pallas_call(layer_kernel, out_shape=(jax.ShapeDtypeStruct((nodes, widt...]
where the time goes in v6:
time: 90 us; the launch traced here: 88.9 us
  Pallas kernels  87.7 us (97%)
  between operations  1.29 us (1%)
    pallas_call x1, Pallas kernels, shards(): pl.pallas_call(layer_kernel, out_shape=(jax.ShapeDtypeStruct((nodes, widt...  85.8 us
    pallas_call x1, Pallas kernels, shards(): pl.pallas_call(copy_kernel, out_shape=tuple((jax.ShapeDtypeStruct(r.shape...  1.82 us

profile of v6, /device:TPU:1, one launch (start us, length us, event | category | flops | bytes accessed | tf_op | source)
XLA Modules:
  0.0 88.9 jit_solution(2260758979916819062)
XLA Ops:
  1.3 85.8 %layer.1 = (bf16[1024,128]{1,0:T(8,128)(2,1)}, f32[4,32,128]{2,1,0:T(8,128)}, bf16[1024,128]{1,0:T(8,128)(2,1)}) custom-call(s32[1]{0:T(128)S(6)} %copy.10.count_ref, bf16[1024,128]{1,0:T(8,128)(2,1)} %features_ref.1, bf16[128,128]{1,0:T(8,128)(2,1)} %weight_ref.1, bf16[96,128,128]{2,1,0:T(8,128)(2,1)} %adj_ref.1, s32[1,96]{1,0:T(1,128)} %bitcast.3, ...), custom_call_target="tpu_custom_call" | custom-call | tf_op jit(solution)/shard_map/layer/pallas_call | solution.py:697
  87.1 1.8 %results.1 = (bf16[1024,128]{1,0:T(8,128)(2,1)}, f32[4,32,128]{2,1,0:T(8,128)}, bf16[1024,128]{1,0:T(8,128)(2,1)}) custom-call(bf16[1024,128]{1,0:T(8,128)(2,1)} %get-tuple-element.9.refs_0_, f32[4,32,128]{2,1,0:T(8,128)} %get-tuple-element.10.refs_1_, bf16[1024,128]{1,0:T(8,128)(2,1)} %get-tuple-element.11.refs_2_), custom_call_target="tpu_custom_call" | custom-call | tf_op jit(solution)/shard_map/results/pallas_call | solution.py:755

commit v7 on v6

--- a/solution.py
+++ b/solution.py
@@ -9,7 +9,8 @@
 BF16, F32 = jnp.bfloat16, jnp.float32
 VMEM_BYTES = 63 * 2**20
 RING = 4
-UNROLL = 8
+UNROLL = 48
+BACK_WIDTHS = (64, 64)
 
 
 class Links:
@@ -230,14 +231,18 @@
     count_ref, features_ref, weight_ref, adj_ref, rows_ref, cols_ref, cot_ref,
     out_ref, weight_grad_ref, feature_grad_ref,
     x_buf, weight_buf, adj, ids_buf, cot_buf, table_buf, table,
-    group_0, group_1, running, parts, relay_buf, from_buf, part2_buf, relay2_buf, from2_buf,
+    group_0, group_1, running, running_0, running_1, parts, relay_buf, from_buf, part2_buf, relay2_buf, from2_buf,
     cot_t, hidden_buf, grad_buf, value_buf, grads_0, grads_1,
     term_buf, term_relay, term_from, term_own, term_got,
-    sums, own_buf, twin_buf, relay3_buf, from3_buf,
+    sums_0, sums_1, own_0, own_1, twin_0, twin_1, relay3_0, relay3_1, from3_0, from3_1,
     out_buf, weight_grad, feature_grad, count_buf, local_sem, send_sem, recv_sem,
 ):
     here = Place()
     group, grads = (group_0, group_1), (grads_0, grads_1)
+    running_back, sums, own_buf = (running_0, running_1), (sums_0, sums_1), (own_0, own_1)
+    twin_buf, relay3_buf = (twin_0, twin_1), (relay3_0, relay3_1)
+    from3_buf = (from3_0, from3_1)
+    offsets = (0, BACK_WIDTHS[0])
     tiles, width, tile = parts.shape[2], parts.shape[3], parts.shape[4]
     slots = adj.shape[0]
     links = Links(send_sem, recv_sem)
@@ -329,9 +334,10 @@
         table_buf[i : i + 1, :] = line
     to_scalars = pltpu.make_async_copy(table_buf, table, local_sem.at[7])
     to_scalars.start()
-    running[slots] = jnp.zeros(running.shape[1:], BF16)
-
-    def tile_pass(source, backward):
+    for sums_to in (running, *running_back):
+        sums_to[slots] = jnp.zeros(sums_to.shape[1:], BF16)
+
+    def tile_pass(source, running, backward, between=lambda: None):
         base = 4 if backward else 0
         contract = ((1,), (0,)) if backward else ((1,), (1,))
 
@@ -354,9 +360,12 @@
                 running[at] = acc.astype(BF16)
             return acc
 
-        lax.fori_loop(0, slots // UNROLL, step, jnp.zeros((width, tile), F32))
-
-    def pick(target, base, block):
+        steps = slots // UNROLL
+        acc = lax.fori_loop(0, steps // 2, step, jnp.zeros(running.shape[1:], F32))
+        between()
+        lax.fori_loop(steps // 2, steps, step, acc)
+
+    def pick(target, running, base, block):
         picked = [running[table[base + 3, block * tiles + t]] for t in range(tiles)]
         for t in range(tiles):
             target[block, t] = picked[t]
@@ -411,7 +420,7 @@
         part2_buf[h, a, d] = first_sums[h][a][d].total().astype(BF16)
 
     def scatter_start(h):
-        lax.fori_loop(0, RING * RING, lambda b, _: (pick(parts.at[h], 0, b), 0)[1], 0)
+        lax.fori_loop(0, RING * RING, lambda b, _: (pick(parts.at[h], running, 0, b), 0)[1], 0)
         for d in (2, 1, 3, 0):
             push_first(h, d)
 
@@ -451,12 +460,15 @@
     gather_done(0)
     to_scalars.wait()
     loads[3].wait()
-    tile_pass(group[0], False)
+
+    def gather_rest():
+        gather_near(1)
+        gather_far(1)
+
+    tile_pass(group[0], running, False, gather_rest)
     scatter_start(0)
-    gather_near(1)
-    gather_far(1)
     gather_done(1)
-    tile_pass(group[1], False)
+    tile_pass(group[1], running, False)
     scatter_start(1)
     scatter_relay(0)
     loads[4].wait()
@@ -485,12 +497,12 @@
             pre_grad = (cot_t[t] * slope).astype(BF16)
             own = jnp.dot(weight, pre_grad, preferred_element_type=F32).astype(BF16)
             for h in feature_halves:
-                grads[h][here.col, t] = own[h * width : (h + 1) * width]
+                grads[h][here.col, t] = own[offsets[h] : offsets[h] + BACK_WIDTHS[h]]
             value_buf[t] = value
             hidden_buf[t] = hidden
             grad_buf[t] = pre_grad
 
-    share_phases = [links.phase(parts.at[h, pl.ds(0, 15)]) for h in feature_halves]
+    share_phases = [links.phase(grads[h].at[pl.ds(0, 15)]) for h in feature_halves]
     one_sems = [[links.semaphore() for _ in range(3)] for _ in feature_halves]
     two_sems = [[links.semaphore() for _ in range(RING)] for _ in feature_halves]
     rest_sems = [links.semaphore() for _ in feature_halves]
@@ -550,12 +562,12 @@
     def shared(h):
         links.wait(rest_sems[h], grads[h].at[pl.ds(0, 8)])
 
-    back_phases = [links.phase(parts.at[h, pl.ds(0, 7)]) for h in feature_halves]
+    back_phases = [links.phase(grads[h].at[pl.ds(0, 7)]) for h in feature_halves]
     passing_3, arrived_3 = ([links.semaphore() for _ in feature_halves] for _ in range(2))
     swapped = [[links.semaphore() for _ in range(RING)] for _ in feature_halves]
     totals = [
         Sum4(
-            links, here.y, lambda k, h=h: own_buf.at[h, k], relay3_buf.at[h], from3_buf.at[h],
+            links, here.y, lambda k, h=h: own_buf[h].at[k], relay3_buf[h], from3_buf[h],
             passing_3[h], arrived_3[h], back_phases[h],
         )
         for h in feature_halves
@@ -563,36 +575,36 @@
     near_order = (2, 1, 3, 0)
 
     def block(h, k, core):
-        return sums.at[h, here.y.at(k) * 2 + core]
+        return sums[h].at[here.y.at(k) * 2 + core]
 
     def back_swap(h):
         for k in near_order:
-            pick(sums.at[h], 4, here.y.at(k) * 2 + 1 - here.core)
+            pick(sums[h], running_back[h], 4, here.y.at(k) * 2 + 1 - here.core)
             links.start(
-                block(h, k, 1 - here.core), twin_buf.at[h, k], here.sibling, swapped[h][k],
+                block(h, k, 1 - here.core), twin_buf[h].at[k], here.sibling, swapped[h][k],
                 back_phases[h],
             )
         for k in near_order:
-            pick(sums.at[h], 4, here.y.at(k) * 2 + here.core)
+            pick(sums[h], running_back[h], 4, here.y.at(k) * 2 + here.core)
 
     def back_push(h):
         pushes = {2: totals[h].push_far, 1: totals[h].push_up, 3: totals[h].push_down}
         for k in near_order:
-            links.wait(swapped[h][k], twin_buf.at[h, k])
-            own = block(h, k, here.core)[...].astype(F32) + twin_buf[h, k].astype(F32)
-            own_buf[h, k] = own.astype(BF16)
+            links.wait(swapped[h][k], twin_buf[h].at[k])
+            own = block(h, k, here.core)[...].astype(F32) + twin_buf[h][k].astype(F32)
+            own_buf[h][k] = own.astype(BF16)
             if k in pushes:
                 pushes[k]()
 
     def back_relay(h):
-        links.wait(passing_3[h], relay3_buf.at[h])
+        links.wait(passing_3[h], relay3_buf[h])
         totals[h].relay()
 
     def back_end(h):
-        links.wait(arrived_3[h], from3_buf.at[h])
+        links.wait(arrived_3[h], from3_buf[h])
         whole = totals[h].total()
         for t in range(tiles):
-            feature_grad[tile_rows(t), pl.ds(h * width, width)] = whole[t].T.astype(BF16)
+            feature_grad[tile_rows(t), pl.ds(offsets[h], BACK_WIDTHS[h])] = whole[t].T.astype(BF16)
 
     for h in feature_halves:
         links.wait(arrived_2[h], from2_buf.at[h])
@@ -624,11 +636,10 @@
     weights.next()
     one_push(1)
     two_relay(0, 0)
-    weights.next()
     one_wait(0, 2)
     two_push(0, 2)
+    weights.next()
     two_push(1, 0)
-    weights.next()
     two_relay(0, 1, 3)
     one_relay(1)
     weights.next()
@@ -638,27 +649,27 @@
     two_relay(1, 0)
     one_wait(1, 2)
     two_push(1, 2)
-    weights.next()
     shared(0)
-    tile_pass(grads[0], True)
+    tile_pass(grads[0], running_0, True)
+    weights.next()
+    two_relay(1, 1, 3)
     back_swap(0)
-    two_relay(1, 1, 3)
-    weights.next()
+    two_relay(1, 2)
     back_push(0)
-    two_relay(1, 2)
+    weights.next()
     shared(1)
-    tile_pass(grads[1], True)
+    tile_pass(grads[1], running_1, True)
+    weights.next()
     back_swap(1)
     back_relay(0)
-    weights.next()
     back_push(1)
     weights.next()
     for t in range(tiles):
         out_buf[tile_rows(t), :] = value_buf[t].T.astype(BF16)
     stores[0].start()
+    weights.next()
+    back_relay(1)
     back_end(0)
-    weights.next()
-    back_relay(1)
     weights.next()
     stores[1].start()
     back_end(1)
@@ -689,6 +700,7 @@
     n_row, n_col = lax.axis_size("row"), lax.axis_size("col")
     tiles, half, member = nodes // tile, width // 2, width // RING
     one = (half, tile)
+    backs = [(back, tile) for back in BACK_WIDTHS]
 
     def vmem(*shape, dtype=BF16):
         return pltpu.VMEM(shape, dtype)
@@ -714,6 +726,7 @@
             vmem(n_row, tiles, *one),
             vmem(n_row, tiles, *one),
             vmem(slots + 1, *one),
+            *(vmem(slots + 1, *back) for back in backs),
             vmem(2, n_col, tiles, *one),
             vmem(2, RING, 2, 2, tiles // 4, *one),
             vmem(2, RING, 2, 2, tiles // 2, *one),
@@ -724,18 +737,17 @@
             vmem(tiles, width, tile),
             vmem(tiles, width, tile),
             vmem(tiles, width, tile, dtype=F32),
-            vmem(n_col, tiles, *one),
-            vmem(n_col, tiles, *one),
+            *(vmem(n_col, tiles, *back) for back in backs),
             vmem(RING, member, width, dtype=F32),
             vmem(2, member // 2, width, dtype=F32),
             vmem(2, member, width, dtype=F32),
             vmem(11, member, width, dtype=F32),
             vmem(5, member, width, dtype=F32),
-            vmem(2, n_row, tiles, *one),
-            vmem(2, RING, tiles, *one),
-            vmem(2, RING, tiles, *one),
-            vmem(2, 2, tiles // 2, *one),
-            vmem(2, 2, tiles, *one),
+            *(vmem(n_row, tiles, *back) for back in backs),
+            *(vmem(RING, tiles, *back) for back in backs),
+            *(vmem(RING, tiles, *back) for back in backs),
+            *(vmem(2, tiles // 2, *back) for back in backs),
+            *(vmem(2, tiles, *back) for back in backs),
             vmem(nodes, width),
             vmem(RING, member, width, dtype=F32),
             vmem(nodes, width),

time: 90 us -> 87.1 us (0.968)
  Pallas kernels: 87.7 us -> 85.5 us
    pallas_call x1, Pallas kernels: 85.8 us -> 83.7 us  [shards(): pl.pallas_call(layer_kernel, out_shape=(jax.ShapeDtypeStruct((nodes, widt...]
where the time goes in v7:
time: 87.1 us; the launch traced here: 86.8 us
  Pallas kernels  85.5 us (98%)
  between operations  1.29 us (1%)
    pallas_call x1, Pallas kernels, shards(): pl.pallas_call(layer_kernel, out_shape=(jax.ShapeDtypeStruct((nodes, widt...  83.7 us
    pallas_call x1, Pallas kernels, shards(): pl.pallas_call(copy_kernel, out_shape=tuple((jax.ShapeDtypeStruct(r.shape...  1.82 us

profile of v7, /device:TPU:1, one launch (start us, length us, event | category | flops | bytes accessed | tf_op | source)
XLA Modules:
  0.0 86.8 jit_solution(7546557123915742888)
XLA Ops:
  1.3 83.7 %layer.1 = (bf16[1024,128]{1,0:T(8,128)(2,1)}, f32[4,32,128]{2,1,0:T(8,128)}, bf16[1024,128]{1,0:T(8,128)(2,1)}) custom-call(s32[1]{0:T(128)S(6)} %copy.10.count_ref, bf16[1024,128]{1,0:T(8,128)(2,1)} %features_ref.1, bf16[128,128]{1,0:T(8,128)(2,1)} %weight_ref.1, bf16[96,128,128]{2,1,0:T(8,128)(2,1)} %adj_ref.1, s32[1,96]{1,0:T(1,128)} %bitcast.3, ...), custom_call_target="tpu_custom_call" | custom-call | tf_op jit(solution)/shard_map/layer/pallas_call | solution.py:709
  84.9 1.8 %results.1 = (bf16[1024,128]{1,0:T(8,128)(2,1)}, f32[4,32,128]{2,1,0:T(8,128)}, bf16[1024,128]{1,0:T(8,128)(2,1)}) custom-call(bf16[1024,128]{1,0:T(8,128)(2,1)} %get-tuple-element.9.refs_0_, f32[4,32,128]{2,1,0:T(8,128)} %get-tuple-element.10.refs_1_, bf16[1024,128]{1,0:T(8,128)(2,1)} %get-tuple-element.11.refs_2_), custom_call_target="tpu_custom_call" | custom-call | tf_op jit(solution)/shard_map/results/pallas_call | solution.py:767

commit v8 on v7

--- a/solution.py
+++ b/solution.py
@@ -651,18 +651,18 @@
     two_push(1, 2)
     shared(0)
     tile_pass(grads[0], running_0, True)
-    weights.next()
     two_relay(1, 1, 3)
     back_swap(0)
     two_relay(1, 2)
+    weights.next()
     back_push(0)
     weights.next()
     shared(1)
     tile_pass(grads[1], running_1, True)
-    weights.next()
     back_swap(1)
     back_relay(0)
     back_push(1)
+    weights.next()
     weights.next()
     for t in range(tiles):
         out_buf[tile_rows(t), :] = value_buf[t].T.astype(BF16)

time: 87.1 us -> 88.1 us (1.011)
  no operation moved by 1% of the time
where the time goes in v8:
time: 88.1 us; the launch traced here: 87.2 us
  Pallas kernels  85.9 us (98%)
  between operations  1.29 us (1%)
    pallas_call x1, Pallas kernels, shards(): pl.pallas_call(layer_kernel, out_shape=(jax.ShapeDtypeStruct((nodes, widt...  84.1 us
    pallas_call x1, Pallas kernels, shards(): pl.pallas_call(copy_kernel, out_shape=tuple((jax.ShapeDtypeStruct(r.shape...  1.82 us

profile of v8, /device:TPU:1, one launch (start us, length us, event | category | flops | bytes accessed | tf_op | source)
XLA Modules:
  0.0 87.2 jit_solution(16570772415813503314)
XLA Ops:
  1.3 84.1 %layer.1 = (bf16[1024,128]{1,0:T(8,128)(2,1)}, f32[4,32,128]{2,1,0:T(8,128)}, bf16[1024,128]{1,0:T(8,128)(2,1)}) custom-call(s32[1]{0:T(128)S(6)} %copy.10.count_ref, bf16[1024,128]{1,0:T(8,128)(2,1)} %features_ref.1, bf16[128,128]{1,0:T(8,128)(2,1)} %weight_ref.1, bf16[96,128,128]{2,1,0:T(8,128)(2,1)} %adj_ref.1, s32[1,96]{1,0:T(1,128)} %bitcast.3, ...), custom_call_target="tpu_custom_call" | custom-call | tf_op jit(solution)/shard_map/layer/pallas_call | solution.py:709
  85.4 1.8 %results.1 = (bf16[1024,128]{1,0:T(8,128)(2,1)}, f32[4,32,128]{2,1,0:T(8,128)}, bf16[1024,128]{1,0:T(8,128)(2,1)}) custom-call(bf16[1024,128]{1,0:T(8,128)(2,1)} %get-tuple-element.9.refs_0_, f32[4,32,128]{2,1,0:T(8,128)} %get-tuple-element.10.refs_1_, bf16[1024,128]{1,0:T(8,128)(2,1)} %get-tuple-element.11.refs_2_), custom_call_target="tpu_custom_call" | custom-call | tf_op jit(solution)/shard_map/results/pallas_call | solution.py:767

commit v9 on v7

--- a/solution.py
+++ b/solution.py
@@ -657,6 +657,9 @@
     two_relay(1, 2)
     back_push(0)
     weights.next()
+    for t in range(tiles):
+        out_buf[tile_rows(t), :] = value_buf[t].T.astype(BF16)
+    stores[0].start()
     shared(1)
     tile_pass(grads[1], running_1, True)
     weights.next()
@@ -664,9 +667,6 @@
     back_relay(0)
     back_push(1)
     weights.next()
-    for t in range(tiles):
-        out_buf[tile_rows(t), :] = value_buf[t].T.astype(BF16)
-    stores[0].start()
     weights.next()
     back_relay(1)
     back_end(0)

time: 87.1 us -> 87.1 us (level)
  no operation moved by 1% of the time
where the time goes in v9:
time: 87.1 us; the launch traced here: 86.8 us
  Pallas kernels  85.5 us (98%)
  between operations  1.29 us (1%)
    pallas_call x1, Pallas kernels, shards(): pl.pallas_call(layer_kernel, out_shape=(jax.ShapeDtypeStruct((nodes, widt...  83.7 us
    pallas_call x1, Pallas kernels, shards(): pl.pallas_call(copy_kernel, out_shape=tuple((jax.ShapeDtypeStruct(r.shape...  1.82 us

profile of v9, /device:TPU:1, one launch (start us, length us, event | category | flops | bytes accessed | tf_op | source)
XLA Modules:
  0.0 86.8 jit_solution(8759392456982766774)
XLA Ops:
  1.3 83.7 %layer.1 = (bf16[1024,128]{1,0:T(8,128)(2,1)}, f32[4,32,128]{2,1,0:T(8,128)}, bf16[1024,128]{1,0:T(8,128)(2,1)}) custom-call(s32[1]{0:T(128)S(6)} %copy.10.count_ref, bf16[1024,128]{1,0:T(8,128)(2,1)} %features_ref.1, bf16[128,128]{1,0:T(8,128)(2,1)} %weight_ref.1, bf16[96,128,128]{2,1,0:T(8,128)(2,1)} %adj_ref.1, s32[1,96]{1,0:T(1,128)} %bitcast.3, ...), custom_call_target="tpu_custom_call" | custom-call | tf_op jit(solution)/shard_map/layer/pallas_call | solution.py:709
  84.9 1.8 %results.1 = (bf16[1024,128]{1,0:T(8,128)(2,1)}, f32[4,32,128]{2,1,0:T(8,128)}, bf16[1024,128]{1,0:T(8,128)(2,1)}) custom-call(bf16[1024,128]{1,0:T(8,128)(2,1)} %get-tuple-element.9.refs_0_, f32[4,32,128]{2,1,0:T(8,128)} %get-tuple-element.10.refs_1_, bf16[1024,128]{1,0:T(8,128)(2,1)} %get-tuple-element.11.refs_2_), custom_call_target="tpu_custom_call" | custom-call | tf_op jit(solution)/shard_map/results/pallas_call | solution.py:767
